TPU v7x, 32 devices: a whole 2x2x4 slice. The times are simulated.
32 devices in a mesh: groups: 2 (over y), strip: 4 (over z), cand: 2 (over x), feat: 2 (over core).
Axes of the slice: x: 2, y: 2, z: 4, core: 2. Of those that a mesh axis runs over, the one named last changes fastest.
Arguments:
- src_pos: float32 [3, 32768], P(None, ('groups', 'strip')), parts along dimension 1, may hold values from -1 to 1
- src_feat: bfloat16 [128, 32768], P('feat', ('groups', 'strip')), parts along dimension 1, may hold values from -10.5 to 10.5
- tgt_pos: float32 [3, 32768], P(None, ('groups', 'strip', 'cand')), parts along dimension 1, may hold values from -0.6 to 1.4
- tgt_feat: bfloat16 [128, 32768], P('feat', ('groups', 'strip', 'cand')), parts along dimension 1, may hold values from -10.5 to 10.5
- displacement: float32 [3, 32768], P(None, ('groups', 'strip')), parts along dimension 1, may hold values from -1 to 1
- sigma_sq: float32 [8], P(('groups', 'strip')), parts along dimension 0, may hold values from 0.5 to 2
- seed_target: int32 [32768], P(('groups', 'strip')), parts along dimension 0, may hold values from 0 to 8191
- counts: int32 [8], P(('groups', 'strip')), parts along dimension 0, may hold values from 512 to 4096
- edges: int32 [8, 32768], P(None, ('groups', 'strip')), parts along dimension 1, may hold values from 0 to 12287, as said below
Outputs:
- new_disp: float32 [3, 32768], P(None, ('groups', 'strip')), parts along dimension 1
- match_mass: float32 [32768], P(('groups', 'strip')), parts along dimension 0
There are 2 independent parts, one for each index of `groups`. A program takes and returns all parts, laid end to end along the dimension named above; each array names one. Nothing has to cross between parts.
Inputs may be any that keep to these rules, and one draw needn't show every extreme that they name: `seed_target`: values of 4096 or more mean that the point has no tie point. `edges`: the strip that an edge names exists, and its slot is below that strip's count; for a live source point at slot i the slot that an edge names lies within 16 of i.
All inputs are finite; a program needn't handle non-finite values.
Results may differ from a plain program's by a relative error of at most 0.0003.
Values may be sent and summed in bfloat16 or wider, within the bound.
No kernel may reach another device: no remote copies, remote signals or barrier semaphores. Data moves between devices by JAX's collectives and lax.ppermute only.
A program may use at most 128 MiB of HBM per device.

v0:
```python
import functools

import jax
import jax.numpy as jnp
from jax import lax
from jax.experimental import pallas as pl
from jax.experimental.pallas import tpu as pltpu
from jax.sharding import PartitionSpec as P

REACH = 16
SWEEPS = 4
EDGES = 8
SPAN = 2 * REACH + 1
LANES = 128
ROWS_WIN = 24
KEEP = LANES - 2 * REACH

feature_scale = 0.18
tie_gain = 3.0
outlier_level = 1.0
strip_offset = 2.0
kernel_scale = 8.0
coherence = 0.1

LOG2E = 1.4426950408889634
VMEM = pl.BlockSpec(memory_space=pltpu.VMEM)
SMEM = pl.BlockSpec(memory_space=pltpu.SMEM)
F32 = jnp.float32
BF16 = jnp.bfloat16


def three_parts(value):
    first = value.astype(BF16).astype(F32)
    rest = value - first
    second = rest.astype(BF16).astype(F32)
    third = (rest - second).astype(BF16).astype(F32)
    return first, second, third


def lane_ids(rows=1):
    return lax.broadcasted_iota(jnp.int32, (rows, LANES), 1)


def prepare_kernel(
    ints, floats, src_pos, disp, tgt_pos, seeds, edges, geo, z_out, disp_out, cols, aug, x_cols, rows
):
    base = ints[0]
    offset = ints[1]
    slots = src_pos.shape[1]
    sigma = floats[0]
    blocks = cols.shape[0] // LANES
    cands = tgt_pos.shape[1]
    scale = 1.0 / (sigma * feature_scale)
    rows[...] = jnp.zeros_like(rows)
    for at in range(blocks):
        here = pl.ds(pl.multiple_of(base + at * LANES, LANES), LANES)
        pos = src_pos[:, here]
        move = disp[:, here]
        z = pos + move
        edge = edges[:, here]
        slot = base + at * LANES + lane_ids()
        segment = edge // slots
        local = edge - segment * slots
        away = jnp.clip(local - slot + REACH, 0, SPAN - 1)
        code = (segment * SPAN + away).astype(F32)
        high = pos.astype(BF16).astype(F32)
        low = pos - high
        for k in range(EDGES):
            rows[k * blocks + at : k * blocks + at + 1, :] = code[k : k + 1, :]
        for c in range(3):
            put = (EDGES + c) * blocks + at
            rows[put : put + 1, :] = high[c : c + 1, :]
            put = (EDGES + 3 + c) * blocks + at
            rows[put : put + 1, :] = low[c : c + 1, :]
            z_out[c, at : at + 1, :] = z[c : c + 1, :]
            disp_out[c, at : at + 1, :] = move[c : c + 1, :]
        first, second, third = three_parts(z * scale)
        norm = jnp.sum(z * z, axis=0, keepdims=True) * (0.5 / sigma)
        level = (norm + outlier_level) * LOG2E
        seed = (seeds[:, here] - offset).astype(F32)
        ones = jnp.ones((3, LANES), F32)
        tile = jnp.concatenate(
            [first, first, second, second, first, third, ones, seed, level]
            + [jnp.zeros((9, LANES), F32)],
            axis=0,
        )
        cols[at * LANES : (at + 1) * LANES, :] = jnp.concatenate(
            [tile.T, jnp.zeros((LANES, LANES - 32), F32)], axis=1
        )
    geo[...] = rows[...].astype(BF16)
    for at in range(cands // LANES):
        here = pl.ds(at * LANES, LANES)
        x = tgt_pos[:, here]
        first, second, third = three_parts(x)
        norm = jnp.sum(x * x, axis=0, keepdims=True) * (-0.5 * scale)
        parts = three_parts(norm)
        aug[:, here] = jnp.concatenate(
            [first, second, first, second, third, first, *parts, jnp.zeros((LANES - 21, LANES), F32)],
            axis=0,
        ).astype(BF16)
        one = jnp.ones((1, LANES), F32)
        gap = jnp.zeros((5, LANES), F32)
        tile = jnp.concatenate(
            [first, one, gap[:4], second, gap, third, gap, jnp.zeros((8, LANES), F32)], axis=0
        )
        x_cols[at * LANES : (at + 1) * LANES, :] = jnp.concatenate(
            [tile.T, jnp.zeros((LANES, LANES - 32), F32)], axis=1
        ).astype(BF16)


def score_kernel(
    ints, src_own, src_other, tgt_own, tgt_other, cols, aug, x_cols, state, left, score, highest, *, chunk, tile
):
    base = ints[0]
    points = cols.shape[0]
    blocks = points // LANES
    cands = aug.shape[1]
    half = src_own.shape[0]
    for at in range(blocks):
        here = pl.ds(pl.multiple_of(base + at * LANES, LANES), LANES)
        down = slice(at * LANES, (at + 1) * LANES)
        both = jnp.concatenate([src_own[:, here], src_other[:, here]], axis=0)
        left[down, 0 : 2 * half] = both.T
        left[down, 2 * half :] = cols[down, :].astype(BF16)
    tiles = cands // tile
    per = tile // LANES
    for t in range(tiles):
        across = slice(t * tile, (t + 1) * tile)
        right = jnp.concatenate([tgt_own[:, across], tgt_other[:, across], aug[:, across]], axis=0)
        for r in range(0, points, chunk):
            product = jnp.dot(left[r : r + chunk, :], right, preferred_element_type=F32)
            score[t, r : r + chunk] = product
            top = product[:, :LANES]
            for q in range(1, per):
                top = jnp.maximum(top, product[:, q * LANES : (q + 1) * LANES])
            highest[r : r + chunk] = top if t == 0 else jnp.maximum(highest[r : r + chunk], top)
    ids = lax.broadcasted_iota(jnp.int32, (1, tile), 1).astype(F32)
    state[...] = jnp.zeros_like(state)
    for r in range(0, points, chunk):
        seed = cols[r : r + chunk, 21:22]
        level = cols[r : r + chunk, 22:23]
        top = jnp.max(highest[r : r + chunk], axis=1, keepdims=True) * (feature_scale * LOG2E)
        peak = jnp.maximum(top, level)
        tied = peak - tie_gain * LOG2E
        total = jnp.zeros((chunk, LANES), F32)
        for t in range(tiles):
            shift = jnp.where(ids + float(t * tile) == seed, tied, peak)
            weight = jnp.exp2(score[t, r : r + chunk] * (feature_scale * LOG2E) - shift)
            high = weight.astype(BF16)
            low = (weight - high.astype(F32)).astype(BF16)
            x = x_cols[t * tile : (t + 1) * tile, :]
            total += jnp.dot(high, x, preferred_element_type=F32)
            total += jnp.dot(low, x, preferred_element_type=F32)
        total = jnp.where(lane_ids() == 4, peak, total)
        highest[r : r + chunk] = total
    for at in range(blocks):
        flat = highest[at * LANES : (at + 1) * LANES, :].T
        summed = flat[0:8] + flat[8:16] + flat[16:24]
        for q in range(5):
            state[q * blocks + at : q * blocks + at + 1, :] = summed[q : q + 1, :]


def merge_kernel(ints, floats, z_ref, *refs):
    *states, terms, mass_out = refs
    blocks = z_ref.shape[1]
    sigma = floats[0]

    def part(ref, q):
        return ref[q * blocks : (q + 1) * blocks, :]

    peak = part(states[0], 4)
    for ref in states[1:]:
        peak = jnp.maximum(peak, part(ref, 4))
    sums = [jnp.zeros((blocks, LANES), F32)] * 4
    for ref in states:
        factor = jnp.exp2(part(ref, 4) - peak)
        sums = [s + part(ref, q) * factor for q, s in enumerate(sums)]
    z = [z_ref[c] for c in range(3)]
    norm = (z[0] * z[0] + z[1] * z[1] + z[2] * z[2]) * (0.5 / sigma)
    slot = ints[0] + LANES * lax.broadcasted_iota(jnp.int32, (blocks, LANES), 0) + lane_ids(blocks)
    live = (slot < ints[2]).astype(F32)
    denom = sums[3] + jnp.exp2((norm + outlier_level) * LOG2E - peak)
    each = live / denom
    mass = sums[3] * each
    diag = mass + coherence * sigma
    inverse = 1.0 / diag
    terms[...] = jnp.zeros_like(terms)
    for c in range(3):
        terms[c * blocks : (c + 1) * blocks, :] = (sums[c] * each - mass * z[c]) * inverse
    terms[3 * blocks : 4 * blocks, :] = mass * inverse
    mass_out[...] = mass


def to_windows(rows, put):
    lane = lane_ids()
    groups = ROWS_WIN // 4
    for w, begin in enumerate((-REACH, KEEP - REACH, 2 * KEEP - REACH, 3 * KEEP - REACH)):
        row = begin // LANES
        start = begin - row * LANES
        first = rows[pl.ds(8 + row, groups, stride=3), :]
        second = rows[pl.ds(9 + row, groups, stride=3), :]
        put(w, pltpu.roll(jnp.where(lane >= start, first, second), LANES - start, 1))


def fill_rows(rows, values):
    blocks = values.shape[0]
    rows[8 : 8 + blocks, :] = values


def pick(value, index):
    return jnp.take_along_axis(value, index, axis=1, mode="promise_in_bounds")


def each_strip(count, body):
    if count <= 4:
        for j in range(count):
            body(j)
    else:
        lax.fori_loop(0, count, lambda j, c: (body(j), c)[1], 0)


def kernels_kernel(ints, *refs, strips, blocks):
    geos = refs[:strips]
    index_out, segment_out, weight_out, wide, rows, codes, places = refs[strips:]
    me = ints[3]
    groups = ROWS_WIN // 4
    lane = lane_ids(8)
    rows[...] = jnp.zeros_like(rows)
    places[0] = jnp.zeros_like(places[0])
    places[strips + 1] = jnp.zeros_like(places[0])

    for d in range(strips):
        wide[...] = geos[d][...].astype(F32)
        j = lax.rem(me + d, strips)

        for k in range(EDGES):
            fill_rows(rows, wide[k * blocks : (k + 1) * blocks, :])

            def put_code(w, value, k=k, j=j):
                codes[j, k, pl.ds(w, groups, stride=4), :] = value

            to_windows(rows, put_code)
        for c in range(3):
            at = (EDGES + c) * blocks
            more = at + 3 * blocks
            fill_rows(rows, wide[at : at + blocks, :] + wide[more : more + blocks, :])

            def put_place(w, value, c=c, j=j):
                places[j + 1, c, pl.ds(w, groups, stride=4), :] = value

            to_windows(rows, put_place)

    def one_strip(j):
        for v in range(ROWS_WIN // 8):
            down = slice(8 * v, 8 * v + 8)
            own = [places[j + 1, c, down, :] for c in range(3)]
            near = [[places[j + g, c, down, :] for c in range(3)] for g in range(3)]
            for k in range(EDGES):
                code = codes[j, k, down, :].astype(jnp.int32)
                later = code >= SPAN
                last = code >= 2 * SPAN
                segment = later.astype(jnp.int32) + last.astype(jnp.int32)
                index = jnp.clip(lane + code - segment * SPAN - REACH, 0, LANES - 1)
                total = None
                for c in range(3):
                    got = jnp.where(
                        last,
                        pick(near[2][c], index),
                        jnp.where(later, pick(near[1][c], index), pick(near[0][c], index)),
                    )
                    gap = own[c] - got
                    if c == 0:
                        gap = gap - strip_offset * (segment - 1).astype(F32)
                    total = gap * gap if total is None else total + gap * gap
                weight_out[j, k, down, :] = jnp.exp(total * (-0.5 / kernel_scale)) * (1.0 / EDGES)
                index_out[j, k, down, :] = index
                segment_out[j, k, down, :] = segment

    each_strip(strips, one_strip)


def sweep_kernel(ints, *refs, strips, blocks):
    terms = refs[:strips]
    index, segment, weight, disp, mass, out = refs[strips : strips + 6]
    rows, base, gain, even, odd, last_rows = refs[strips + 6 :]
    me = ints[3]
    core = ints[4]
    groups = ROWS_WIN // 4
    parts = ROWS_WIN // 8
    lane = lane_ids(8)
    rows[...] = jnp.zeros_like(rows)
    for field in (even, odd):
        field[...] = jnp.zeros_like(field)

    for d in range(strips):
        j = lax.rem(me + d, strips)
        for q in range(4):
            fill_rows(rows, terms[d][q * blocks : (q + 1) * blocks, :])

            def put(w, value, q=q, j=j):
                if q < 3:
                    base[j, q, pl.ds(w, groups, stride=4), :] = value
                    even[j + 1, q, pl.ds(8 + w, groups, stride=4), :] = value
                else:
                    gain[j, pl.ds(w, groups, stride=4), :] = value

            to_windows(rows, put)

    def spread(field, j, v):
        down = slice(8 * v, 8 * v + 8)
        inner = slice(8 * v + 8, 8 * v + 16)
        near = [[field[j + g, c, inner, :] for c in range(3)] for g in range(3)]
        sums = [None] * 3
        for k in range(EDGES):
            at = index[j, k, down, :]
            part = segment[j, k, down, :]
            later = part >= 1
            last = part >= 2
            size = weight[j, k, down, :]
            for c in range(3):
                got = jnp.where(
                    last,
                    pick(near[2][c], at),
                    jnp.where(later, pick(near[1][c], at), pick(near[0][c], at)),
                )
                sums[c] = size * got if sums[c] is None else sums[c] + size * got
        return sums

    for sweep in range(SWEEPS):
        now, after = (even, odd) if sweep % 2 == 0 else (odd, even)
        wanted = SWEEPS - sweep

        def one_strip(j, now=now, after=after, wanted=wanted):
            @pl.when(jnp.abs(me - j) <= wanted)
            def _():
                for v in range(parts):
                    down = slice(8 * v, 8 * v + 8)
                    inner = slice(8 * v + 8, 8 * v + 16)
                    sums = spread(now, j, v)
                    for c in range(3):
                        after[j + 1, c, inner, :] = base[j, c, down, :] - gain[j, down, :] * sums[c]
                for c in range(3):
                    for v in range(parts):
                        at = 8 * v + 8
                        here = after[j + 1, c, at : at + 8, :]
                        before = after[j + 1, c, at - 1 : at + 7, :]
                        behind = after[j + 1, c, at + 1 : at + 9, :]
                        after[j + 1, c, at : at + 8, :] = jnp.where(
                            lane < REACH,
                            pltpu.roll(before, 2 * REACH, 1),
                            jnp.where(lane >= LANES - REACH, pltpu.roll(behind, KEEP, 1), here),
                        )

        each_strip(strips, one_strip)

    field = even if SWEEPS % 2 == 0 else odd
    for v in range(parts):
        sums = spread(field, me, v)
        for c in range(3):
            last_rows[c, 8 * v : 8 * v + 8, :] = sums[c] + field[me + 1, c, 8 * v + 8 : 8 * v + 16, :]
    wide_lane = lane_ids()
    many = ROWS_WIN // 4
    for c in range(3):
        for i in range(3):
            begin = LANES * i - KEEP * i + REACH
            first = last_rows[c, pl.ds(i, many, stride=4), :]
            second = last_rows[c, pl.ds(i + 1, many, stride=4), :]
            held = KEEP - (LANES - KEEP) * i
            value = jnp.where(
                wide_lane < held,
                pltpu.roll(first, LANES - begin, 1),
                pltpu.roll(second, (held - REACH) % LANES, 1),
            )
            rows[pl.ds(i, many, stride=3), :] = value
        slot = ints[0] + LANES * lax.broadcasted_iota(jnp.int32, (blocks, LANES), 0) + lane_ids(blocks)
        rows[0:blocks, :] = disp[c] + jnp.where(slot < ints[2], rows[0:blocks, :], 0.0)
        for at in range(blocks - 1):
            out[c : c + 1, at * LANES : (at + 1) * LANES] = rows[pl.ds(core + at, 1), :]
    rows[0:blocks, :] = mass[...]
    for at in range(blocks - 1):
        out[3:4, at * LANES : (at + 1) * LANES] = rows[pl.ds(core + at, 1), :]


def around(array, axis):
    count = lax.axis_size(axis)
    return [array] + [
        lax.ppermute(array, axis, [((i + d) % count, i) for i in range(count)]) for d in range(1, count)
    ]


def on_device(
    src_pos, src_feat, tgt_pos, tgt_feat, displacement, sigma_sq, seed_target, counts, edges
):
    slots = src_pos.shape[1]
    cands = tgt_pos.shape[1]
    strips = lax.axis_size("strip")
    half = slots // 2
    points = half + LANES
    blocks = points // LANES
    core = lax.axis_index("feat")
    base = core * (half - LANES)
    ints = jnp.stack(
        [base, lax.axis_index("cand") * cands, counts[0], lax.axis_index("strip"), core]
    ).astype(jnp.int32)

    src_other = around(src_feat, "feat")[1]
    tgt_other = around(tgt_feat, "feat")[1]

    geo_rows = 16 * ((14 * blocks + 15) // 16)
    geo, z, disp, cols, aug, x_cols = pl.pallas_call(
        prepare_kernel,
        name="prepare",
        out_shape=(
            jax.ShapeDtypeStruct((geo_rows, LANES), BF16),
            jax.ShapeDtypeStruct((3, blocks, LANES), F32),
            jax.ShapeDtypeStruct((3, blocks, LANES), F32),
            jax.ShapeDtypeStruct((points, LANES), F32),
            jax.ShapeDtypeStruct((LANES, cands), BF16),
            jax.ShapeDtypeStruct((cands, LANES), BF16),
        ),
        in_specs=[SMEM, SMEM] + [VMEM] * 5,
        out_specs=(VMEM,) * 6,
        scratch_shapes=[pltpu.VMEM((geo_rows, LANES), F32)],
    )(ints, sigma_sq, src_pos, displacement, tgt_pos, seed_target.reshape(1, slots), edges)

    geos = around(geo, "strip")

    chunk = points // 8
    tile = 256
    state_rows = 8 * ((5 * blocks + 7) // 8)
    state = pl.pallas_call(
        functools.partial(score_kernel, chunk=chunk, tile=tile),
        name="score",
        out_shape=jax.ShapeDtypeStruct((state_rows, LANES), F32),
        in_specs=[SMEM] + [VMEM] * 7,
        out_specs=VMEM,
        scratch_shapes=[
            pltpu.VMEM((points, 2 * LANES), BF16),
            pltpu.VMEM((cands // tile, points, tile), F32),
            pltpu.VMEM((points, LANES), F32),
        ],
        compiler_params=pltpu.CompilerParams(vmem_limit_bytes=48 << 20),
    )(ints, src_feat, src_other, tgt_feat, tgt_other, cols, aug, x_cols)

    states = around(state, "cand")
    term_rows = 8 * ((4 * blocks + 7) // 8)
    terms, mass = pl.pallas_call(
        merge_kernel,
        name="merge",
        out_shape=(
            jax.ShapeDtypeStruct((term_rows, LANES), F32),
            jax.ShapeDtypeStruct((blocks, LANES), F32),
        ),
        in_specs=[SMEM, SMEM] + [VMEM] * (1 + len(states)),
        out_specs=(VMEM, VMEM),
    )(ints, sigma_sq, z, *states)

    all_terms = around(terms, "strip")

    shape = (strips, EDGES, ROWS_WIN, LANES)
    index, segment, weight = pl.pallas_call(
        functools.partial(kernels_kernel, strips=strips, blocks=blocks),
        name="neighbours",
        out_shape=(
            jax.ShapeDtypeStruct(shape, jnp.int32),
            jax.ShapeDtypeStruct(shape, jnp.int32),
            jax.ShapeDtypeStruct(shape, F32),
        ),
        in_specs=[SMEM] + [VMEM] * strips,
        out_specs=(VMEM,) * 3,
        scratch_shapes=[
            pltpu.VMEM((geo_rows, LANES), F32),
            pltpu.VMEM((ROWS_WIN + 16, LANES), F32),
            pltpu.VMEM(shape, F32),
            pltpu.VMEM((strips + 2, 3, ROWS_WIN, LANES), F32),
        ],
    )(ints, *geos)

    field_shape = (strips + 2, 3, ROWS_WIN + 16, LANES)
    part = pl.pallas_call(
        functools.partial(sweep_kernel, strips=strips, blocks=blocks),
        name="sweeps",
        out_shape=jax.ShapeDtypeStruct((4, half), F32),
        in_specs=[SMEM] + [VMEM] * (strips + 5),
        out_specs=VMEM,
        scratch_shapes=[
            pltpu.VMEM((ROWS_WIN + 16, LANES), F32),
            pltpu.VMEM((strips, 3, ROWS_WIN, LANES), F32),
            pltpu.VMEM((strips, ROWS_WIN, LANES), F32),
            pltpu.VMEM(field_shape, F32),
            pltpu.VMEM(field_shape, F32),
            pltpu.VMEM((3, ROWS_WIN + 8, LANES), F32),
        ],
    )(ints, *all_terms, index, segment, weight, disp, mass)

    whole = lax.all_gather(part, "feat", axis=1, tiled=True)
    return (whole[0:3], whole[3])


def solution(mesh):
    in_specs = (
        P(None, ("groups", "strip")),
        P("feat", ("groups", "strip")),
        P(None, ("groups", "strip", "cand")),
        P("feat", ("groups", "strip", "cand")),
        P(None, ("groups", "strip")),
        P(("groups", "strip")),
        P(("groups", "strip")),
        P(("groups", "strip")),
        P(None, ("groups", "strip")),
    )
    out_specs = (P(None, ("groups", "strip")), P(("groups", "strip")))
    return jax.shard_map(
        on_device, mesh=mesh, in_specs=in_specs, out_specs=out_specs, check_vma=False
    )
```

profile of v0, /device:TPU:0, one launch (start us, length us, event | category | flops | bytes accessed | tf_op | source)
XLA Modules:
  0.0 54.6 jit_solution(12001623536312076041)
XLA Ops:
  2.5 0.7 %stack.19.ints = s32[5]{0:T(128)} concatenate(s32[1]{0:T(128)} %bitcast, s32[1]{0:T(128)} %bitcast.1, s32[1]{0:T(128)S(6)} %copy.13, s32[1]{0:T(128)} %bitcast.2, s32[1]{0:T(128)} %bitcast.3), dimensions={0} | concatenate | bytes 40 | tf_op jit(solution)/shard_map/stack | solution.py:402
  3.2 2.8 %prepare.1 = (bf16[240,128]{1,0:T(8,128)(2,1)}, f32[3,17,128]{2,1,0:T(8,128)}, f32[3,17,128]{2,1,0:T(8,128)}, f32[2176,128]{1,0:T(8,128)}, bf16[128,2048]{1,0:T(8,128)(2,1)}, /*index=5*/bf16[2048,128]{1,0:T(8,128)(2,1)}) custom-call(s32[5]{0:T(128)} %stack.19.ints, f32[1]{0:T(128)S(6)} %copy.12.floats, f32[3,4096]{1,0:T(4,128)} %src_pos.1, f32[3,4096]{1,0:T(4,128)} %disp.1, ...), custom_call_target="tpu_custom_call" | custom-call | tf_op jit(solution)/shard_map/prepare/pallas_call | solution.py:410
  6.0 3.0 %collective-permute-start.8 = (bf16[240,128]{1,0:T(8,128)(2,1)}, bf16[240,128]{1,0:T(8,128)(2,1)S(1)}, u32[]{:S(2)}, u32[]{:S(2)}) collective-permute-start(bf16[240,128]{1,0:T(8,128)(2,1)} %get-tuple-element.18.refs_0_), channel_id=1, source_target_pairs={{12,0},{0,4},{4,8},{8,12},{13,1},{1,5},{5,9},{9,13},{14,2},{2,6},{... | collective-permute-start | bytes 184328 | tf_op jit(solution)/shard_map/ppermute | solution.py:387
  9.0 1.2 %copy-done = f32[2176,128]{1,0:T(8,128)S(1)} copy-done((f32[2176,128]{1,0:T(8,128)S(1)}, f32[2176,128]{1,0:T(8,128)}, u32[]{:S(2)}) %copy-start) | copy-done | bytes 1114136
  10.3 1.0 %copy-done.1 = bf16[64,4096]{1,0:T(8,128)(2,1)S(1)} copy-done((bf16[64,4096]{1,0:T(8,128)(2,1)S(1)}, bf16[64,4096]{1,0:T(8,128)(2,1)}, u32[]{:S(2)}) %copy-start.1) | copy-done | bytes 524312
  11.3 1.0 %copy-done.2 = bf16[128,2048]{1,0:T(8,128)(2,1)S(1)} copy-done((bf16[128,2048]{1,0:T(8,128)(2,1)S(1)}, bf16[128,2048]{1,0:T(8,128)(2,1)}, u32[]{:S(2)}) %copy-start.2) | copy-done | bytes 524312
  12.4 1.0 %copy-done.3 = bf16[2048,128]{1,0:T(8,128)(2,1)S(1)} copy-done((bf16[2048,128]{1,0:T(8,128)(2,1)S(1)}, bf16[2048,128]{1,0:T(8,128)(2,1)}, u32[]{:S(2)}) %copy-start.3) | copy-done | bytes 524312
  13.4 0.9 %copy-done.4 = bf16[64,2048]{1,0:T(8,128)(2,1)S(1)} copy-done((bf16[64,2048]{1,0:T(8,128)(2,1)S(1)}, bf16[64,2048]{1,0:T(8,128)(2,1)}, u32[]{:S(2)}) %copy-start.4) | copy-done | bytes 262168
  14.4 0.7 %copy-done.6 = s32[5]{0:T(128)S(1)} copy-done((s32[5]{0:T(128)S(1)}, s32[5]{0:T(128)}, u32[]{:S(2)}) %copy-start.6) | copy-done | bytes 44
  15.0 9.6 %score.1.refs_0_ = f32[88,128]{1,0:T(8,128)S(1)} custom-call(s32[5]{0:T(128)S(1)} %copy-done.6, bf16[64,4096]{1,0:T(8,128)(2,1)S(1)} %copy-done.1, bf16[64,4096]{1,0:T(8,128)(2,1)S(1)} %collective-permute-done.src_other, bf16[64,2048]{1,0:T(8,128)(2,1)S(1)} %copy-done.4, bf16[64,2048]{1,0:T(8,128)(2,1)S(1)} %collective-permute-done.1.tgt_other, ...), custom_call_target="tpu_custom_call" | custom-call | tf_op jit(solution)/shard_map/score/pallas_call | solution.py:431
  24.6 1.6 %collective-permute-start.2 = (f32[88,128]{1,0:T(8,128)S(1)}, f32[88,128]{1,0:T(8,128)S(1)}, u32[]{:S(2)}, u32[]{:S(2)}) collective-permute-start(f32[88,128]{1,0:T(8,128)S(1)} %score.1.refs_0_), channel_id=1, source_target_pairs={{2,0},{0,2},{3,1},{1,3},{6,4},{4,6},{7,5},{5,7},{10,8},{8,10},{11,... | collective-permute-start | bytes 135176 | tf_op jit(solution)/shard_map/ppermute | solution.py:387
  26.2 2.6 %collective-permute-start.7 = (bf16[240,128]{1,0:T(8,128)(2,1)S(1)}, bf16[240,128]{1,0:T(8,128)(2,1)S(1)}, u32[]{:S(2)}, u32[]{:S(2)}) collective-permute-start(bf16[240,128]{1,0:T(8,128)(2,1)S(1)} %copy-done.7), channel_id=1, source_target_pairs={{8,0},{12,4},{0,8},{4,12},{9,1},{13,5},{1,9},{5,13},{10,2},{14,6},... | collective-permute-start | bytes 184328 | tf_op jit(solution)/shard_map/ppermute | solution.py:387
  28.8 1.4 %collective-permute-start.6 = (bf16[240,128]{1,0:T(8,128)(2,1)S(1)}, bf16[240,128]{1,0:T(8,128)(2,1)S(1)}, u32[]{:S(2)}, u32[]{:S(2)}) collective-permute-start(bf16[240,128]{1,0:T(8,128)(2,1)S(1)} %copy-done.7), channel_id=1, source_target_pairs={{4,0},{8,4},{12,8},{0,12},{5,1},{9,5},{13,9},{1,13},{6,2},{10,6},{... | collective-permute-start | bytes 184328 | tf_op jit(solution)/shard_map/ppermute | solution.py:387
  30.1 0.6 %copy-done.11 = f32[88,128]{1,0:T(8,128)} copy-done((f32[88,128]{1,0:T(8,128)}, f32[88,128]{1,0:T(8,128)S(1)}, u32[]{:S(2)}) %copy-start.11) | copy-done | bytes 45080
  30.7 1.5 %merge.1 = (f32[72,128]{1,0:T(8,128)}, f32[17,128]{1,0:T(8,128)}) custom-call(s32[5]{0:T(128)} %stack.19.ints, f32[1]{0:T(128)S(6)} %copy.12.floats, f32[3,17,128]{2,1,0:T(8,128)} %get-tuple-element.13.z_ref, f32[88,128]{1,0:T(8,128)} %copy-done.5, f32[88,128]{1,0:T(8,128)} %copy-done.11), custom_call_target="tpu_custom_call" | custom-call | tf_op jit(solution)/shard_map/merge/pallas_call | solution.py:447
  32.2 0.7 %collective-permute-start.5 = (f32[72,128]{1,0:T(8,128)}, f32[72,128]{1,0:T(8,128)S(1)}, u32[]{:S(2)}, u32[]{:S(2)}) collective-permute-start(f32[72,128]{1,0:T(8,128)} %get-tuple-element.17.refs_0_), channel_id=1, source_target_pairs={{12,0},{0,4},{4,8},{8,12},{13,1},{1,5},{5,9},{9,13},{14,2},{2,6},{... | collective-permute-start | bytes 110600 | tf_op jit(solution)/shard_map/ppermute | solution.py:387
  33.5 2.9 %collective-permute-start.3 = (f32[72,128]{1,0:T(8,128)}, f32[72,128]{1,0:T(8,128)S(1)}, u32[]{:S(2)}, u32[]{:S(2)}) collective-permute-start(f32[72,128]{1,0:T(8,128)} %get-tuple-element.17.refs_0_), channel_id=1, source_target_pairs={{4,0},{8,4},{12,8},{0,12},{5,1},{9,5},{13,9},{1,13},{6,2},{10,6},{... | collective-permute-start | bytes 110600 | tf_op jit(solution)/shard_map/ppermute | solution.py:387
  36.4 0.6 %copy-done.9 = bf16[240,128]{1,0:T(8,128)(2,1)} copy-done((bf16[240,128]{1,0:T(8,128)(2,1)}, bf16[240,128]{1,0:T(8,128)(2,1)S(1)}, u32[]{:S(2)}) %copy-start.9) | copy-done | bytes 61464
  37.0 0.6 %copy-done.10 = bf16[240,128]{1,0:T(8,128)(2,1)} copy-done((bf16[240,128]{1,0:T(8,128)(2,1)}, bf16[240,128]{1,0:T(8,128)(2,1)S(1)}, u32[]{:S(2)}) %copy-start.10) | copy-done | bytes 61464
  37.6 3.4 %neighbours.1 = (s32[4,8,24,128]{3,2,1,0:T(8,128)}, s32[4,8,24,128]{3,2,1,0:T(8,128)}, f32[4,8,24,128]{3,2,1,0:T(8,128)}) custom-call(s32[5]{0:T(128)} %stack.19.ints, bf16[240,128]{1,0:T(8,128)(2,1)} %get-tuple-element.18.refs_0_, bf16[240,128]{1,0:T(8,128)(2,1)} %copy-done.10, bf16[240,128]{1,0:T(8,128)(2,1)} %copy-done.9, bf16[240,128]{1,0:T(8,128)(2,1)} %copy-done.8), custom_call_target="tpu_custom_call" | custom-call | tf_op jit(solution)/shard_map/neighbours/pallas_call | solution.py:461
  41.7 9.6 %sweeps.1 = f32[4,2048]{1,0:T(4,128)} custom-call(s32[5]{0:T(128)} %stack.19.ints, f32[72,128]{1,0:T(8,128)} %get-tuple-element.17.refs_0_, f32[72,128]{1,0:T(8,128)} %copy-done.14, f32[72,128]{1,0:T(8,128)} %copy-done.13, f32[72,128]{1,0:T(8,128)} %copy-done.12, s32[4,8,24,128]{3,2,1,0:T(8,128)} %get-tuple-element.19.refs_4_, ...), custom_call_target="tpu_custom_call" | custom-call | tf_op jit(solution)/shard_map/sweeps/pallas_call | solution.py:480
  51.3 2.1 %all_gather.3 = f32[4,4096]{1,0:T(4,128)S(1)} all-gather(f32[4,2048]{1,0:T(4,128)} %sweeps.1), channel_id=1, replica_groups=mesh['groups'=2,'strip'=4,'cand'=2,'feat'=2] {'feat'}, dimensions={1}, use_global_device_ids=true | all-gather | bytes 98304 | tf_op jit(solution)/shard_map/all_gather | solution.py:496
  53.4 0.6 %slice.9 = f32[1,4096]{1,0:T(1,128)} slice(f32[4,4096]{1,0:T(4,128)S(1)} %all_gather.3), slice={[3:4], [0:4096]} | slice | bytes 32768 | tf_op jit(solution)/shard_map/slice | solution.py:497
  54.0 0.6 %copy.14 = f32[3,4096]{1,0:T(4,128)} copy(f32[3,4096]{1,0:T(4,128)S(1)} %bitcast.7) | data formatting | bytes 98304
  (33 shorter events, 1.8 us)
Async XLA Ops:
  0.6 8.4 %collective-permute-start = (bf16[64,4096]{1,0:T(8,128)(2,1)}, bf16[64,4096]{1,0:T(8,128)(2,1)S(1)}, u32[]{:S(2)}, u32[]{:S(2)}) collective-permute-start(bf16[64,4096]{1,0:T(8,128)(2,1)} %src_own.1), channel_id=1, source_target_pairs={{1,0},{0,1},{3,2},{2,3},{5,4},{4,5},{7,6},{6,7},{9,8},{8,9},{11,10... | collective-permute-start | bytes 1572872 | tf_op jit(solution)/shard_map/ppermute | solution.py:387
  1.1 7.9 %collective-permute-start.1 = (bf16[64,2048]{1,0:T(8,128)(2,1)}, bf16[64,2048]{1,0:T(8,128)(2,1)S(1)}, u32[]{:S(2)}, u32[]{:S(2)}) collective-permute-start(bf16[64,2048]{1,0:T(8,128)(2,1)} %tgt_own.1), channel_id=1, source_target_pairs={{1,0},{0,1},{3,2},{2,3},{5,4},{4,5},{7,6},{6,7},{9,8},{8,9},{11,10... | collective-permute-start | bytes 786440 | tf_op jit(solution)/shard_map/ppermute | solution.py:387
  6.0 27.4 %collective-permute-start.8 = (bf16[240,128]{1,0:T(8,128)(2,1)}, bf16[240,128]{1,0:T(8,128)(2,1)S(1)}, u32[]{:S(2)}, u32[]{:S(2)}) collective-permute-start(bf16[240,128]{1,0:T(8,128)(2,1)} %get-tuple-element.18.refs_0_), channel_id=1, source_target_pairs={{12,0},{0,4},{4,8},{8,12},{13,1},{1,5},{5,9},{9,13},{14,2},{2,6},{... | collective-permute-start | bytes 184328 | tf_op jit(solution)/shard_map/ppermute | solution.py:387
  9.0 1.2 %copy-start = (f32[2176,128]{1,0:T(8,128)S(1)}, f32[2176,128]{1,0:T(8,128)}, u32[]{:S(2)}) copy-start(f32[2176,128]{1,0:T(8,128)} %get-tuple-element.14.cols) | copy-start | bytes 3342340
  10.3 1.0 %copy-start.1 = (bf16[64,4096]{1,0:T(8,128)(2,1)S(1)}, bf16[64,4096]{1,0:T(8,128)(2,1)}, u32[]{:S(2)}) copy-start(bf16[64,4096]{1,0:T(8,128)(2,1)} %src_own.1) | copy-start | bytes 1572868
  11.3 1.0 %copy-start.2 = (bf16[128,2048]{1,0:T(8,128)(2,1)S(1)}, bf16[128,2048]{1,0:T(8,128)(2,1)}, u32[]{:S(2)}) copy-start(bf16[128,2048]{1,0:T(8,128)(2,1)} %get-tuple-element.15.aug) | copy-start | bytes 1572868
  12.4 1.0 %copy-start.3 = (bf16[2048,128]{1,0:T(8,128)(2,1)S(1)}, bf16[2048,128]{1,0:T(8,128)(2,1)}, u32[]{:S(2)}) copy-start(bf16[2048,128]{1,0:T(8,128)(2,1)} %get-tuple-element.16.x_cols) | copy-start | bytes 1572868
  13.4 0.9 %copy-start.4 = (bf16[64,2048]{1,0:T(8,128)(2,1)S(1)}, bf16[64,2048]{1,0:T(8,128)(2,1)}, u32[]{:S(2)}) copy-start(bf16[64,2048]{1,0:T(8,128)(2,1)} %tgt_own.1) | copy-start | bytes 786436
  14.4 0.7 %copy-start.6 = (s32[5]{0:T(128)S(1)}, s32[5]{0:T(128)}, u32[]{:S(2)}) copy-start(s32[5]{0:T(128)} %stack.19.ints) | copy-start | bytes 64
  15.0 11.1 %copy-start.7 = (bf16[240,128]{1,0:T(8,128)(2,1)S(1)}, bf16[240,128]{1,0:T(8,128)(2,1)}, u32[]{:S(2)}) copy-start(bf16[240,128]{1,0:T(8,128)(2,1)} %get-tuple-element.18.refs_0_) | copy-start | bytes 184324
  24.6 5.5 %copy-start.5 = (f32[88,128]{1,0:T(8,128)}, f32[88,128]{1,0:T(8,128)S(1)}, u32[]{:S(2)}) copy-start(f32[88,128]{1,0:T(8,128)S(1)} %score.1.refs_0_) | copy-start | bytes 135172
  24.6 5.5 %collective-permute-start.2 = (f32[88,128]{1,0:T(8,128)S(1)}, f32[88,128]{1,0:T(8,128)S(1)}, u32[]{:S(2)}, u32[]{:S(2)}) collective-permute-start(f32[88,128]{1,0:T(8,128)S(1)} %score.1.refs_0_), channel_id=1, source_target_pairs={{2,0},{0,2},{3,1},{1,3},{6,4},{4,6},{7,5},{5,7},{10,8},{8,10},{11,... | collective-permute-start | bytes 135176 | tf_op jit(solution)/shard_map/ppermute | solution.py:387
  26.2 10.2 %collective-permute-start.7 = (bf16[240,128]{1,0:T(8,128)(2,1)S(1)}, bf16[240,128]{1,0:T(8,128)(2,1)S(1)}, u32[]{:S(2)}, u32[]{:S(2)}) collective-permute-start(bf16[240,128]{1,0:T(8,128)(2,1)S(1)} %copy-done.7), channel_id=1, source_target_pairs={{8,0},{12,4},{0,8},{4,12},{9,1},{13,5},{1,9},{5,13},{10,2},{14,6},... | collective-permute-start | bytes 184328 | tf_op jit(solution)/shard_map/ppermute | solution.py:387
  28.8 7.6 %collective-permute-start.6 = (bf16[240,128]{1,0:T(8,128)(2,1)S(1)}, bf16[240,128]{1,0:T(8,128)(2,1)S(1)}, u32[]{:S(2)}, u32[]{:S(2)}) collective-permute-start(bf16[240,128]{1,0:T(8,128)(2,1)S(1)} %copy-done.7), channel_id=1, source_target_pairs={{4,0},{8,4},{12,8},{0,12},{5,1},{9,5},{13,9},{1,13},{6,2},{10,6},{... | collective-permute-start | bytes 184328 | tf_op jit(solution)/shard_map/ppermute | solution.py:387
  30.1 0.6 %copy-start.11 = (f32[88,128]{1,0:T(8,128)}, f32[88,128]{1,0:T(8,128)S(1)}, u32[]{:S(2)}) copy-start(f32[88,128]{1,0:T(8,128)S(1)} %collective-permute-done.2.refs_1_) | copy-start | bytes 135172
  32.2 8.8 %collective-permute-start.5 = (f32[72,128]{1,0:T(8,128)}, f32[72,128]{1,0:T(8,128)S(1)}, u32[]{:S(2)}, u32[]{:S(2)}) collective-permute-start(f32[72,128]{1,0:T(8,128)} %get-tuple-element.17.refs_0_), channel_id=1, source_target_pairs={{12,0},{0,4},{4,8},{8,12},{13,1},{1,5},{5,9},{9,13},{14,2},{2,6},{... | collective-permute-start | bytes 110600 | tf_op jit(solution)/shard_map/ppermute | solution.py:387
  32.9 8.1 %collective-permute-start.4 = (f32[72,128]{1,0:T(8,128)}, f32[72,128]{1,0:T(8,128)S(1)}, u32[]{:S(2)}, u32[]{:S(2)}) collective-permute-start(f32[72,128]{1,0:T(8,128)} %get-tuple-element.17.refs_0_), channel_id=1, source_target_pairs={{8,0},{12,4},{0,8},{4,12},{9,1},{13,5},{1,9},{5,13},{10,2},{14,6},... | collective-permute-start | bytes 110600 | tf_op jit(solution)/shard_map/ppermute | solution.py:387
  33.5 2.9 %copy-start.8 = (bf16[240,128]{1,0:T(8,128)(2,1)}, bf16[240,128]{1,0:T(8,128)(2,1)S(1)}, u32[]{:S(2)}) copy-start(bf16[240,128]{1,0:T(8,128)(2,1)S(1)} %collective-permute-done.8.refs_3_) | copy-start | bytes 184324
  33.5 7.6 %collective-permute-start.3 = (f32[72,128]{1,0:T(8,128)}, f32[72,128]{1,0:T(8,128)S(1)}, u32[]{:S(2)}, u32[]{:S(2)}) collective-permute-start(f32[72,128]{1,0:T(8,128)} %get-tuple-element.17.refs_0_), channel_id=1, source_target_pairs={{4,0},{8,4},{12,8},{0,12},{5,1},{9,5},{13,9},{1,13},{6,2},{10,6},{... | collective-permute-start | bytes 110600 | tf_op jit(solution)/shard_map/ppermute | solution.py:387
  36.4 0.6 %copy-start.9 = (bf16[240,128]{1,0:T(8,128)(2,1)}, bf16[240,128]{1,0:T(8,128)(2,1)S(1)}, u32[]{:S(2)}) copy-start(bf16[240,128]{1,0:T(8,128)(2,1)S(1)} %collective-permute-done.7.refs_2_) | copy-start | bytes 184324
  37.0 0.6 %copy-start.10 = (bf16[240,128]{1,0:T(8,128)(2,1)}, bf16[240,128]{1,0:T(8,128)(2,1)S(1)}, u32[]{:S(2)}) copy-start(bf16[240,128]{1,0:T(8,128)(2,1)S(1)} %collective-permute-done.6.refs_1_) | copy-start | bytes 184324
  41.0 0.6 %copy-start.12 = (f32[72,128]{1,0:T(8,128)}, f32[72,128]{1,0:T(8,128)S(1)}, u32[]{:S(2)}) copy-start(f32[72,128]{1,0:T(8,128)S(1)} %collective-permute-done.5.refs_3_) | copy-start | bytes 110596
  41.0 0.6 %copy-start.13 = (f32[72,128]{1,0:T(8,128)}, f32[72,128]{1,0:T(8,128)S(1)}, u32[]{:S(2)}) copy-start(f32[72,128]{1,0:T(8,128)S(1)} %collective-permute-done.4.refs_2_) | copy-start | bytes 110596
  41.1 0.6 %copy-start.14 = (f32[72,128]{1,0:T(8,128)}, f32[72,128]{1,0:T(8,128)S(1)}, u32[]{:S(2)}) copy-start(f32[72,128]{1,0:T(8,128)S(1)} %collective-permute-done.3.refs_1_) | copy-start | bytes 110596
where the time goes:
time: 55.1 us; the launch traced here: 54.6 us
  Pallas kernels  26.9 us (49%)
  starting transfers between devices  13.2 us (24%)
  local copies, waits for them, and re-layouts  10.4 us (19%)
  blocking collectives  2.05 us (4%)
  between operations  2 us (4%)
    ppermute x9, starting transfers between devices, around(): lax.ppermute(array, axis, [((i + d) % count, i) for i in range(count)])  13.2 us
    pallas_call x1, Pallas kernels, on_device(): pl.pallas_call(functools.partial(sweep_kernel, strips=strips, blocks=bloc...  9.63 us
    pallas_call x1, Pallas kernels, on_device(): pl.pallas_call(functools.partial(score_kernel, chunk=chunk, tile=tile), n...  9.55 us
    unnamed x31, local copies, waits for them, and re-layouts  9.08 us
    pallas_call x1, Pallas kernels, on_device(): pl.pallas_call(functools.partial(kernels_kernel, strips=strips, blocks=bl...  3.41 us
    pallas_call x1, Pallas kernels, on_device(): pl.pallas_call(prepare_kernel, name='prepare', out_shape=(jax.ShapeDtypeS...  2.82 us
    all_gather x1, blocking collectives, on_device(): whole = lax.all_gather(part, 'feat', axis=1, tiled=True)  2.05 us
    pallas_call x1, Pallas kernels, on_device(): pl.pallas_call(merge_kernel, name='merge', out_shape=(jax.ShapeDtypeStruc...  1.52 us
  transfers between devices with their start and end apart: 9, of which 0 were waited for; matrix products, arithmetic and copies ran while one was open for 1% of the time, Pallas kernels for 32%

commit v1 on v0

v1 whole, which is shorter than its diff:
```python
import functools

import jax
import jax.numpy as jnp
from jax import lax
from jax.experimental import pallas as pl
from jax.experimental.pallas import tpu as pltpu
from jax.sharding import PartitionSpec as P

REACH = 16
SWEEPS = 4
EDGES = 8
SPAN = 2 * REACH + 1
LANES = 128
ROWS_WIN = 24
KEEP = LANES - 2 * REACH

feature_scale = 0.18
tie_gain = 3.0
outlier_level = 1.0
strip_offset = 2.0
kernel_scale = 8.0
coherence = 0.1

LOG2E = 1.4426950408889634
VMEM = pl.BlockSpec(memory_space=pltpu.VMEM)
F32 = jnp.float32
BF16 = jnp.bfloat16


def first_slot(slots):
    return lax.axis_index("feat") * (slots // 2 - LANES)


def three_parts(value):
    first = value.astype(BF16).astype(F32)
    rest = value - first
    second = rest.astype(BF16).astype(F32)
    third = (rest - second).astype(BF16).astype(F32)
    return first, second, third


def lane_ids(rows=1):
    return lax.broadcasted_iota(jnp.int32, (rows, LANES), 1)


def copies_in(sources, targets, done):
    copies = [
        pltpu.make_async_copy(source, target, done.at[n])
        for n, (source, target) in enumerate(zip(sources, targets))
    ]
    for copy in copies:
        copy.start()
    return copies


def geometry_kernel(
    far_pos, far_disp, far_edges, far_counts, far_sigma, geo, z_out, disp_out, src_pos, disp, edges, counts, sigma, rows, done
):
    slots = src_pos.shape[1]
    base = first_slot(slots)
    blocks = z_out.shape[1]
    copies = copies_in(
        [far_pos, far_disp, far_edges, far_counts, far_sigma], [src_pos, disp, edges, counts, sigma], done
    )
    rows[...] = jnp.zeros_like(rows)
    for copy in copies:
        copy.wait()
    for at in range(blocks):
        here = pl.ds(pl.multiple_of(base + at * LANES, LANES), LANES)
        pos = src_pos[:, here]
        move = disp[:, here]
        z = pos + move
        edge = edges[:, here]
        slot = base + at * LANES + lane_ids()
        segment = edge // slots
        local = edge - segment * slots
        away = jnp.clip(local - slot + REACH, 0, SPAN - 1)
        code = (segment * SPAN + away).astype(F32)
        high = pos.astype(BF16).astype(F32)
        low = pos - high
        for k in range(EDGES):
            rows[k * blocks + at : k * blocks + at + 1, :] = code[k : k + 1, :]
        for c in range(3):
            put = (EDGES + c) * blocks + at
            rows[put : put + 1, :] = high[c : c + 1, :]
            put = (EDGES + 3 + c) * blocks + at
            rows[put : put + 1, :] = low[c : c + 1, :]
            z_out[c, at : at + 1, :] = z[c : c + 1, :]
            disp_out[c, at : at + 1, :] = move[c : c + 1, :]
    live = (slot_ids(slots, blocks) < counts[0]).astype(F32)
    z_out[3] = live
    z_out[4] = jnp.full((blocks, LANES), sigma[0], F32)
    disp_out[3] = live
    geo[...] = rows[...].astype(BF16)


def score_kernel(*refs, chunk, tile):
    far, state, near = refs[:9], refs[9], refs[10:19]
    cols, aug, x_cols, left, score, highest, done = refs[19:]
    slots = far[1].shape[1]
    points = cols.shape[0]
    mine = pl.ds(pl.multiple_of(first_slot(slots), LANES), points)
    sources = [*far[:5], far[5].at[:, mine], far[6].at[:, mine], far[7], far[8]]
    copies = copies_in(sources, near, done)
    for copy in copies[:5]:
        copy.wait()
    prepare(*near[:5], cols, aug, x_cols)
    for copy in copies[5:]:
        copy.wait()
    score_all(*near[5:], cols, aug, x_cols, state, left, score, highest, chunk=chunk, tile=tile)


def prepare(sigmas, src_pos, disp, tgt_pos, seeds, cols, aug, x_cols):
    slots = src_pos.shape[1]
    base = first_slot(slots)
    sigma = sigmas[0]
    blocks = cols.shape[0] // LANES
    cands = tgt_pos.shape[1]
    offset = lax.axis_index("cand") * cands
    scale = 1.0 / (sigma * feature_scale)
    for at in range(blocks):
        here = pl.ds(pl.multiple_of(base + at * LANES, LANES), LANES)
        z = src_pos[:, here] + disp[:, here]
        first, second, third = three_parts(z * scale)
        norm = jnp.sum(z * z, axis=0, keepdims=True) * (0.5 / sigma)
        level = (norm + outlier_level) * LOG2E
        seed = (seeds[:, here] - offset).astype(F32)
        ones = jnp.ones((3, LANES), F32)
        tile = jnp.concatenate(
            [first, first, second, second, first, third, ones, seed, level]
            + [jnp.zeros((9, LANES), F32)],
            axis=0,
        )
        cols[at * LANES : (at + 1) * LANES, :] = jnp.concatenate(
            [tile.T, jnp.zeros((LANES, LANES - 32), F32)], axis=1
        )
    for at in range(cands // LANES):
        here = pl.ds(at * LANES, LANES)
        x = tgt_pos[:, here]
        first, second, third = three_parts(x)
        norm = jnp.sum(x * x, axis=0, keepdims=True) * (-0.5 * scale)
        parts = three_parts(norm)
        aug[:, here] = jnp.concatenate(
            [first, second, first, second, third, first, *parts, jnp.zeros((LANES - 21, LANES), F32)],
            axis=0,
        ).astype(BF16)
        one = jnp.ones((1, LANES), F32)
        gap = jnp.zeros((5, LANES), F32)
        tile = jnp.concatenate(
            [first, one, gap[:4], second, gap, third, gap, jnp.zeros((8, LANES), F32)], axis=0
        )
        x_cols[at * LANES : (at + 1) * LANES, :] = jnp.concatenate(
            [tile.T, jnp.zeros((LANES, LANES - 32), F32)], axis=1
        ).astype(BF16)


def score_all(src_own, src_other, tgt_own, tgt_other, cols, aug, x_cols, state, left, score, highest, *, chunk, tile):
    points = cols.shape[0]
    blocks = points // LANES
    cands = aug.shape[1]
    half = src_own.shape[0]
    for at in range(blocks):
        down = slice(at * LANES, (at + 1) * LANES)
        both = jnp.concatenate([src_own[:, down], src_other[:, down]], axis=0)
        left[down, 0 : 2 * half] = both.T
        left[down, 2 * half :] = cols[down, :].astype(BF16)
    tiles = cands // tile
    per = tile // LANES
    for t in range(tiles):
        across = slice(t * tile, (t + 1) * tile)
        right = jnp.concatenate([tgt_own[:, across], tgt_other[:, across], aug[:, across]], axis=0)
        for r in range(0, points, chunk):
            product = jnp.dot(left[r : r + chunk, :], right, preferred_element_type=F32)
            score[t, r : r + chunk] = product
            top = product[:, :LANES]
            for q in range(1, per):
                top = jnp.maximum(top, product[:, q * LANES : (q + 1) * LANES])
            highest[r : r + chunk] = top if t == 0 else jnp.maximum(highest[r : r + chunk], top)
    ids = lax.broadcasted_iota(jnp.int32, (1, tile), 1).astype(F32)
    state[...] = jnp.zeros_like(state)
    for r in range(0, points, chunk):
        seed = cols[r : r + chunk, 21:22]
        level = cols[r : r + chunk, 22:23]
        top = jnp.max(highest[r : r + chunk], axis=1, keepdims=True) * (feature_scale * LOG2E)
        peak = jnp.maximum(top, level)
        tied = peak - tie_gain * LOG2E
        total = jnp.zeros((chunk, LANES), F32)
        for t in range(tiles):
            shift = jnp.where(ids + float(t * tile) == seed, tied, peak)
            weight = jnp.exp2(score[t, r : r + chunk] * (feature_scale * LOG2E) - shift)
            high = weight.astype(BF16)
            low = (weight - high.astype(F32)).astype(BF16)
            x = x_cols[t * tile : (t + 1) * tile, :]
            total += jnp.dot(high, x, preferred_element_type=F32)
            total += jnp.dot(low, x, preferred_element_type=F32)
        total = jnp.where(lane_ids() == 4, peak, total)
        highest[r : r + chunk] = total
    for at in range(blocks):
        flat = highest[at * LANES : (at + 1) * LANES, :].T
        summed = flat[0:8] + flat[8:16] + flat[16:24]
        for q in range(5):
            state[q * blocks + at : q * blocks + at + 1, :] = summed[q : q + 1, :]


def slot_ids(slots, blocks):
    rows = lax.broadcasted_iota(jnp.int32, (blocks, LANES), 0)
    return first_slot(slots) + LANES * rows + lane_ids(blocks)


def merge_kernel(z_ref, *refs):
    *states, _, terms, mass_out = refs
    blocks = z_ref.shape[1]
    live = z_ref[3]
    sigma = z_ref[4]

    def part(ref, q):
        return ref[q * blocks : (q + 1) * blocks, :]

    peak = part(states[0], 4)
    for ref in states[1:]:
        peak = jnp.maximum(peak, part(ref, 4))
    sums = [jnp.zeros((blocks, LANES), F32)] * 4
    for ref in states:
        factor = jnp.exp2(part(ref, 4) - peak)
        sums = [s + part(ref, q) * factor for q, s in enumerate(sums)]
    z = [z_ref[c] for c in range(3)]
    norm = (z[0] * z[0] + z[1] * z[1] + z[2] * z[2]) * (0.5 / sigma)
    denom = sums[3] + jnp.exp2((norm + outlier_level) * LOG2E - peak)
    each = live / denom
    mass = sums[3] * each
    diag = mass + coherence * sigma
    inverse = 1.0 / diag
    terms[...] = jnp.zeros_like(terms)
    for c in range(3):
        terms[c * blocks : (c + 1) * blocks, :] = (sums[c] * each - mass * z[c]) * inverse
    terms[3 * blocks : 4 * blocks, :] = mass * inverse
    mass_out[...] = mass


def to_windows(rows, put):
    lane = lane_ids()
    groups = ROWS_WIN // 4
    for w, begin in enumerate((-REACH, KEEP - REACH, 2 * KEEP - REACH, 3 * KEEP - REACH)):
        row = begin // LANES
        start = begin - row * LANES
        first = rows[pl.ds(8 + row, groups, stride=3), :]
        second = rows[pl.ds(9 + row, groups, stride=3), :]
        put(w, pltpu.roll(jnp.where(lane >= start, first, second), LANES - start, 1))


def fill_rows(rows, values):
    blocks = values.shape[0]
    rows[8 : 8 + blocks, :] = values


def pick(value, index):
    return jnp.take_along_axis(value, index, axis=1, mode="promise_in_bounds")


def each_strip(count, body):
    if count <= 4:
        for j in range(count):
            body(j)
    else:
        lax.fori_loop(0, count, lambda j, c: (body(j), c)[1], 0)


def packed(values):
    first, second, third = (value.astype(jnp.int32) for value in values)
    third = third + (1 << 20)
    return (first << 11) + (third >> 10), (second << 11) + (third & 1023)


def unpacked(words):
    first, second = words
    third = ((first & 2047) << 10) + (second & 1023) - (1 << 20)
    return [value.astype(F32) for value in (first >> 11, second >> 11, third)]


def picked(words, index, later, last, ends):
    low, high = ends
    got = []
    for w in range(len(words[1])):
        value = pick(words[1][w], index)
        if not low:
            value = jnp.where(later, value, pick(words[0][w], index))
        if not high:
            value = jnp.where(last, pick(words[2][w], index), value)
        got.append(value)
    return got


def ends_of(j, strips):
    return (j == 0, j == strips - 1) if isinstance(j, int) else (False, False)


def kernels_kernel(*refs, strips, blocks):
    geos = refs[:strips]
    index_out, segment_out, weight_out, wide, rows, codes, raw, places = refs[strips:]
    groups = ROWS_WIN // 4
    lane = lane_ids(8)
    rows[...] = jnp.zeros_like(rows)
    places[0] = jnp.zeros_like(places[0])
    places[strips + 1] = jnp.zeros_like(places[0])
    unit = float(1 << 19)

    for d in range(strips):
        wide[...] = geos[d][...].astype(F32)
        j = lax.rem(lax.axis_index("strip") + d, strips)

        for k in range(EDGES):
            fill_rows(rows, wide[k * blocks : (k + 1) * blocks, :])

            def put_code(w, value, k=k, j=j):
                codes[j, k, pl.ds(w, groups, stride=4), :] = value

            to_windows(rows, put_code)
        for c in range(3):
            at = (EDGES + c) * blocks
            more = at + 3 * blocks
            fill_rows(rows, wide[at : at + blocks, :] + wide[more : more + blocks, :])

            def put_place(w, value, c=c):
                raw[c, pl.ds(w, groups, stride=4), :] = value

            to_windows(rows, put_place)
        for q, word in enumerate(packed([raw[c] * unit for c in range(3)])):
            places[j + 1, q] = word

    def one_strip(j):
        ends = ends_of(j, strips)
        for v in range(ROWS_WIN // 8):
            down = slice(8 * v, 8 * v + 8)
            near = [[places[j + g, q, down, :] for q in range(2)] for g in range(3)]
            own = unpacked(near[1])
            for k in range(EDGES):
                code = codes[j, k, down, :].astype(jnp.int32)
                later = code >= SPAN
                last = code >= 2 * SPAN
                segment = later.astype(jnp.int32) + last.astype(jnp.int32)
                index = jnp.clip(lane + code - segment * SPAN - REACH, 0, LANES - 1)
                got = unpacked(picked(near, index, later, last, ends))
                gaps = [(own[c] - got[c]) * (1.0 / unit) for c in range(3)]
                gaps[0] = gaps[0] - strip_offset * (segment - 1).astype(F32)
                total = gaps[0] * gaps[0] + gaps[1] * gaps[1] + gaps[2] * gaps[2]
                weight_out[j, k, down, :] = jnp.exp(total * (-0.5 / kernel_scale)) * (1.0 / EDGES)
                index_out[j, k, down, :] = index
                segment_out[j, k, down, :] = segment

    each_strip(strips, one_strip)


FIELD_UNIT = float(1 << 20) / 17.5


def sweep_kernel(*refs, strips, blocks):
    terms = refs[:strips]
    index, segment, weight, disp, out = refs[strips : strips + 5]
    rows, base, raw, field, last_rows = refs[strips + 5 :]
    me = lax.axis_index("strip")
    core = lax.axis_index("feat")
    groups = ROWS_WIN // 4
    parts = ROWS_WIN // 8
    lane = lane_ids(8)
    rows[...] = jnp.zeros_like(rows)
    raw[...] = jnp.zeros_like(raw)
    field[0] = jnp.zeros_like(field[0])
    field[strips + 1] = jnp.zeros_like(field[0])

    for d in range(strips):
        j = lax.rem(lax.axis_index("strip") + d, strips)
        for q in range(4):
            fill_rows(rows, terms[d][q * blocks : (q + 1) * blocks, :])

            def put(w, value, q=q, j=j):
                base[j, q, pl.ds(w, groups, stride=4), :] = value

            to_windows(rows, put)
        words = packed([base[j, c] * FIELD_UNIT for c in range(3)])
        for q in range(2):
            field[j + 1, q] = words[q]

    def spread(j, v):
        down = slice(8 * v, 8 * v + 8)
        ends = ends_of(j, strips)
        near = [[field[j + g, q, down, :] for q in range(2)] for g in range(3)]
        sums = [jnp.zeros((8, LANES), F32)] * 3
        for k in range(EDGES):
            part = segment[j, k, down, :]
            got = unpacked(picked(near, index[j, k, down, :], part >= 1, part >= 2, ends))
            size = weight[j, k, down, :]
            sums = [s + size * g for s, g in zip(sums, got)]
        return [s * (1.0 / FIELD_UNIT) for s in sums]

    beyond = jnp.where(lane < LANES // 2, lane + KEEP, lane - KEEP) & (LANES - 1)

    def renew(j):
        for v in range(parts):
            for q in range(2):
                at = 8 * v + 8
                before = raw[j, q, at - 1 : at + 7, :]
                behind = raw[j, q, at + 1 : at + 9, :]
                margin = pick(jnp.where(lane < LANES // 2, behind, before), beyond)
                kept = (lane >= REACH) & (lane < LANES - REACH)
                field[j + 1, q, 8 * v : 8 * v + 8, :] = jnp.where(kept, raw[j, q, at : at + 8, :], margin)

    for sweep in range(SWEEPS):
        wanted = SWEEPS - sweep

        def one_strip(j, wanted=wanted):
            for v in range(parts):
                down = slice(8 * v, 8 * v + 8)
                sums = spread(j, v)
                fresh = [base[j, c, down, :] - base[j, 3, down, :] * sums[c] for c in range(3)]
                words = packed([value * FIELD_UNIT for value in fresh])
                for q in range(2):
                    raw[j, q, 8 * v + 8 : 8 * v + 16, :] = words[q]
                if wanted == 1:

                    @pl.when(me == j)
                    def _():
                        for c in range(3):
                            last_rows[c, down, :] = fresh[c]

        def near_strip(j, body, wanted=wanted):
            if strips <= 4 and wanted > 1:
                body(j)
            else:
                pl.when(jnp.abs(me - j) <= wanted)(lambda: body(j))

        each_strip(strips, lambda j: near_strip(j, one_strip))
        each_strip(strips, lambda j: near_strip(j, renew))

    for v in range(parts):
        down = slice(8 * v, 8 * v + 8)
        sums = spread(me, v)
        for c in range(3):
            last_rows[c, down, :] = sums[c] + last_rows[c, down, :]
    wide_lane = lane_ids()
    live = disp[3] > 0.5
    for c in range(3):
        for i in range(3):
            begin = LANES * i - KEEP * i + REACH
            first = last_rows[c, pl.ds(i, groups, stride=4), :]
            second = last_rows[c, pl.ds(i + 1, groups, stride=4), :]
            held = KEEP - (LANES - KEEP) * i
            value = jnp.where(
                wide_lane < held,
                pltpu.roll(first, LANES - begin, 1),
                pltpu.roll(second, (held - REACH) % LANES, 1),
            )
            rows[pl.ds(i, groups, stride=3), :] = value
        rows[0:blocks, :] = disp[c] + jnp.where(live, rows[0:blocks, :], 0.0)
        for at in range(blocks - 1):
            out[c : c + 1, at * LANES : (at + 1) * LANES] = rows[pl.ds(core + at, 1), :]


def takes(microseconds):
    return pl.CostEstimate(flops=int(microseconds * 1.15e9), bytes_accessed=0, transcendentals=0)


def whole_kernel(part, part_far, mass, mass_far, out, mass_out):
    is_first = lax.axis_index("feat") == 0
    blocks = mass.shape[0]
    half = blocks - 1
    wide = part.shape[1]
    out[:, 0:wide] = jnp.where(is_first, part[...], part_far[...])
    out[:, wide:] = jnp.where(is_first, part_far[...], part[...])
    mass_out[0:half, :] = jnp.where(is_first, mass[0:half, :], mass_far[0:half, :])
    mass_out[half:, :] = jnp.where(is_first, mass_far[1:blocks, :], mass[1:blocks, :])


def around(array, axis):
    count = lax.axis_size(axis)
    return [array] + [
        lax.ppermute(array, axis, [((i + d) % count, i) for i in range(count)]) for d in range(1, count)
    ]


def on_device(
    src_pos, src_feat, tgt_pos, tgt_feat, displacement, sigma_sq, seed_target, counts, edges
):
    slots = src_pos.shape[1]
    cands = tgt_pos.shape[1]
    strips = lax.axis_size("strip")
    half = slots // 2
    points = half + LANES
    blocks = points // LANES
    small = pltpu.CompilerParams(vmem_limit_bytes=12 << 20)

    src_other = around(src_feat, "feat")[1]
    tgt_other = around(tgt_feat, "feat")[1]

    geo_rows = 16 * ((14 * blocks + 15) // 16)
    hbm = pl.BlockSpec(memory_space=pltpu.HBM)
    own = (src_pos, displacement, edges)
    scalars = [pltpu.SMEM((1,), jnp.int32), pltpu.SMEM((1,), F32)]
    geo, z, disp = pl.pallas_call(
        geometry_kernel,
        name="geometry",
        out_shape=(
            jax.ShapeDtypeStruct((geo_rows, LANES), BF16),
            jax.ShapeDtypeStruct((5, blocks, LANES), F32),
            jax.ShapeDtypeStruct((4, blocks, LANES), F32),
        ),
        in_specs=[hbm] * 5,
        out_specs=(VMEM,) * 3,
        scratch_shapes=[pltpu.VMEM(array.shape, array.dtype) for array in own]
        + scalars
        + [pltpu.VMEM((geo_rows, LANES), F32), pltpu.SemaphoreType.DMA((5,))],
        compiler_params=pltpu.CompilerParams(vmem_limit_bytes=(64 << 20) - (64 << 10)),
        cost_estimate=takes(2),
    )(*own, counts, sigma_sq)
    geos = around(geo, "strip")

    arrays = (src_pos, displacement, tgt_pos, seed_target.reshape(1, slots))
    features = (src_feat, src_other, tgt_feat, tgt_other)
    tile = 256
    state_rows = 8 * ((5 * blocks + 7) // 8)
    mine = pltpu.VMEM((src_feat.shape[0], points), BF16)
    theirs = pltpu.VMEM(tgt_feat.shape, BF16)
    state = pl.pallas_call(
        functools.partial(score_kernel, chunk=points // 8, tile=tile),
        name="score",
        out_shape=jax.ShapeDtypeStruct((state_rows, LANES), F32),
        in_specs=[hbm] * 9,
        out_specs=VMEM,
        scratch_shapes=scalars[1:]
        + [pltpu.VMEM(array.shape, array.dtype) for array in arrays]
        + [mine, mine, theirs, theirs]
        + [
            pltpu.VMEM((points, LANES), F32),
            pltpu.VMEM((LANES, cands), BF16),
            pltpu.VMEM((cands, LANES), BF16),
            pltpu.VMEM((points, 2 * LANES), BF16),
            pltpu.VMEM((cands // tile, points, tile), F32),
            pltpu.VMEM((points, LANES), F32),
            pltpu.SemaphoreType.DMA((9,)),
        ],
        compiler_params=pltpu.CompilerParams(vmem_limit_bytes=60 << 20),
        cost_estimate=takes(10),
    )(sigma_sq, *arrays, *features)

    shape = (strips, EDGES, ROWS_WIN, LANES)
    index, segment, weight = pl.pallas_call(
        functools.partial(kernels_kernel, strips=strips, blocks=blocks),
        name="neighbours",
        out_shape=(
            jax.ShapeDtypeStruct(shape, jnp.int32),
            jax.ShapeDtypeStruct(shape, jnp.int32),
            jax.ShapeDtypeStruct(shape, F32),
        ),
        in_specs=[VMEM] * strips,
        out_specs=(VMEM,) * 3,
        scratch_shapes=[
            pltpu.VMEM((geo_rows, LANES), F32),
            pltpu.VMEM((ROWS_WIN + 16, LANES), F32),
            pltpu.VMEM(shape, F32),
            pltpu.VMEM((3, ROWS_WIN, LANES), F32),
            pltpu.VMEM((strips + 2, 2, ROWS_WIN, LANES), jnp.int32),
        ],
        compiler_params=small,
        cost_estimate=takes(2),
    )(*geos)

    states = around(state, "cand")
    term_rows = 8 * ((4 * blocks + 7) // 8)
    terms, mass = pl.pallas_call(
        merge_kernel,
        name="merge",
        out_shape=(
            jax.ShapeDtypeStruct((term_rows, LANES), F32),
            jax.ShapeDtypeStruct((blocks, LANES), F32),
        ),
        in_specs=[VMEM] * (1 + len(states)) + [pl.BlockSpec(memory_space=pl.ANY)],
        out_specs=(VMEM, VMEM),
        compiler_params=small,
        cost_estimate=takes(0.5),
    )(z, *states, weight)

    all_terms = around(terms, "strip")
    mass_far = around(mass, "feat")[1]

    part = pl.pallas_call(
        functools.partial(sweep_kernel, strips=strips, blocks=blocks),
        name="sweeps",
        out_shape=jax.ShapeDtypeStruct((3, half), F32),
        in_specs=[VMEM] * (strips + 4),
        out_specs=VMEM,
        scratch_shapes=[
            pltpu.VMEM((ROWS_WIN + 16, LANES), F32),
            pltpu.VMEM((strips, 4, ROWS_WIN, LANES), F32),
            pltpu.VMEM((strips, 2, ROWS_WIN + 16, LANES), jnp.int32),
            pltpu.VMEM((strips + 2, 2, ROWS_WIN, LANES), jnp.int32),
            pltpu.VMEM((3, ROWS_WIN + 8, LANES), F32),
        ],
        compiler_params=small,
        cost_estimate=takes(7),
    )(*all_terms, index, segment, weight, disp)

    new_disp, mass_whole = pl.pallas_call(
        whole_kernel,
        name="whole",
        out_shape=(
            jax.ShapeDtypeStruct((3, slots), F32),
            jax.ShapeDtypeStruct((slots // LANES, LANES), F32),
        ),
        in_specs=[VMEM] * 4,
        out_specs=(VMEM, VMEM),
        compiler_params=small,
        cost_estimate=takes(0.5),
    )(part, around(part, "feat")[1], mass, mass_far)
    return (new_disp, mass_whole.reshape(slots))


def solution(mesh):
    in_specs = (
        P(None, ("groups", "strip")),
        P("feat", ("groups", "strip")),
        P(None, ("groups", "strip", "cand")),
        P("feat", ("groups", "strip", "cand")),
        P(None, ("groups", "strip")),
        P(("groups", "strip")),
        P(("groups", "strip")),
        P(("groups", "strip")),
        P(None, ("groups", "strip")),
    )
    out_specs = (P(None, ("groups", "strip")), P(("groups", "strip")))
    return jax.shard_map(
        on_device, mesh=mesh, in_specs=in_specs, out_specs=out_specs, check_vma=False
    )
```

time: 55.1 us -> 40.4 us (0.73)
  local copies, waits for them, and re-layouts: 10.4 us -> 0.02 us
  Pallas kernels: 26.9 us -> 19.5 us
  waiting for transfers between devices: 0.02 us -> 4.85 us
  blocking collectives: 2.05 us -> 0 us
  starting transfers between devices: 13.2 us -> 13.8 us
    unnamed x31 -> x8, local copies, waits for them, and re-layouts: 9.08 us -> 0.02 us
    pallas_call x1, Pallas kernels: 9.63 us -> 4.55 us  [on_device(): pl.pallas_call(functools.partial(sweep_kernel, strips=strips, blocks=bloc...]
    ppermute x9 -> x11, waiting for transfers between devices: 0.02 us -> 4.85 us  [around(): lax.ppermute(array, axis, [((i + d) % count, i) for i in range(count)])]
    pallas_call x1, Pallas kernels: 3.41 us -> 1.31 us  [on_device(): pl.pallas_call(functools.partial(kernels_kernel, strips=strips, blocks=bl...]
    all_gather x1 -> x0, blocking collectives: 2.05 us -> none  [on_device(): whole = lax.all_gather(part, 'feat', axis=1, tiled=True)]
    pallas_call x1, Pallas kernels: 1.52 us -> 0.04 us  [on_device(): pl.pallas_call(merge_kernel, name='merge', out_shape=(jax.ShapeDtypeStruc...]
    pallas_call x2 -> x3, Pallas kernels: 12.4 us -> 13.6 us  [the longest x1 11.2 us: on_device(): pl.pallas_call(functools.partial(score_kernel, chunk=points // 8, tile=ti...]
    another operation x1 -> x0, local copies, waits for them, and re-layouts: 0.68 us -> none  [on_device(): jnp.stack([base, lax.axis_index('cand') * cands, counts[0], lax.axis_inde...]
  transfers between devices with their start and end apart: 9 -> 11, of which waited for: 0 -> 4; matrix products, arithmetic and copies ran while one was open for 1% -> 0% of each run, Pallas kernels for 32% -> 36%
where the time goes in v1:
time: 40.4 us; the launch traced here: 40.2 us
  Pallas kernels  19.5 us (48%)
  starting transfers between devices  13.8 us (34%)
  waiting for transfers between devices  4.85 us (12%)
  between operations  2.01 us (5%)
    ppermute x11, starting transfers between devices, around(): lax.ppermute(array, axis, [((i + d) % count, i) for i in range(count)])  13.8 us
    pallas_call x1, Pallas kernels, on_device(): pl.pallas_call(functools.partial(score_kernel, chunk=points // 8, tile=ti...  11.2 us
    ppermute x11, waiting for transfers between devices, around(): lax.ppermute(array, axis, [((i + d) % count, i) for i in range(count)])  4.85 us
    pallas_call x1, Pallas kernels, on_device(): pl.pallas_call(functools.partial(sweep_kernel, strips=strips, blocks=bloc...  4.55 us
    pallas_call x1, Pallas kernels, on_device(): pl.pallas_call(geometry_kernel, name='geometry', out_shape=(jax.ShapeDtyp...  1.81 us
    pallas_call x1, Pallas kernels, on_device(): pl.pallas_call(functools.partial(kernels_kernel, strips=strips, blocks=bl...  1.31 us
  transfers between devices with their start and end apart: 11, of which 4 were waited for; matrix products, arithmetic and copies ran while one was open for 0% of the time, Pallas kernels for 36%

profile of v1, /device:TPU:0, one launch (start us, length us, event | category | flops | bytes accessed | tf_op | source)
XLA Modules:
  0.0 40.2 jit_solution(12371316324561200992)
XLA Ops:
  0.6 0.5 %collective-permute-start = (bf16[64,4096]{1,0:T(8,128)(2,1)}, bf16[64,4096]{1,0:T(8,128)(2,1)}, u32[]{:S(2)}, u32[]{:S(2)}) collective-permute-start(bf16[64,4096]{1,0:T(8,128)(2,1)} %refs_5_.1), channel_id=1, source_target_pairs={{1,0},{0,1},{3,2},{2,3},{5,4},{4,5},{7,6},{6,7},{9,8},{8,9},{11,10... | collective-permute-start | bytes 1572872 | tf_op jit(solution)/shard_map/ppermute | solution.py:477
  1.1 0.1 collective-permute-start.1
  2.5 1.8 %geometry.1 = (bf16[240,128]{1,0:T(8,128)(2,1)}, f32[5,17,128]{2,1,0:T(8,128)}, f32[4,17,128]{2,1,0:T(8,128)}) custom-call(f32[3,4096]{1,0:T(4,128)} %refs_1_.1, f32[3,4096]{1,0:T(4,128)} %refs_2_.1, s32[8,4096]{1,0:T(8,128)} %far_edges.1, s32[1]{0:T(128)S(6)} %copy.12.far_counts, f32[1]{0:T(128)S(6)} %copy.11.far_sigma.refs_0_), custom_call_target="tpu_custom_call" | custom-call | flops 2300000000 | tf_op jit(solution)/shard_map/geometry/pallas_call | solution.py:499
  4.3 3.1 %collective-permute-start.5 = (bf16[240,128]{1,0:T(8,128)(2,1)}, bf16[240,128]{1,0:T(8,128)(2,1)S(1)}, u32[]{:S(2)}, u32[]{:S(2)}) collective-permute-start(bf16[240,128]{1,0:T(8,128)(2,1)} %get-tuple-element.13.refs_0_), channel_id=1, source_target_pairs={{12,0},{0,4},{4,8},{8,12},{13,1},{1,5},{5,9},{9,13},{14,2},{2,6},{... | collective-permute-start | bytes 184328 | tf_op jit(solution)/shard_map/ppermute | solution.py:477
  7.4 2.6 %collective-permute-start.4 = (bf16[240,128]{1,0:T(8,128)(2,1)}, bf16[240,128]{1,0:T(8,128)(2,1)S(1)}, u32[]{:S(2)}, u32[]{:S(2)}) collective-permute-start(bf16[240,128]{1,0:T(8,128)(2,1)} %get-tuple-element.13.refs_0_), channel_id=1, source_target_pairs={{8,0},{12,4},{0,8},{4,12},{9,1},{13,5},{1,9},{5,13},{10,2},{14,6},... | collective-permute-start | bytes 184328 | tf_op jit(solution)/shard_map/ppermute | solution.py:477
  10.0 1.3 %collective-permute-start.3 = (bf16[240,128]{1,0:T(8,128)(2,1)}, bf16[240,128]{1,0:T(8,128)(2,1)S(1)}, u32[]{:S(2)}, u32[]{:S(2)}) collective-permute-start(bf16[240,128]{1,0:T(8,128)(2,1)} %get-tuple-element.13.refs_0_), channel_id=1, source_target_pairs={{4,0},{8,4},{12,8},{0,12},{5,1},{9,5},{13,9},{1,13},{6,2},{10,6},{... | collective-permute-start | bytes 184328 | tf_op jit(solution)/shard_map/ppermute | solution.py:477
  11.3 0.0 collective-permute-done.1.refs_8_
  11.3 11.2 %score.1.refs_0_ = f32[88,128]{1,0:T(8,128)} custom-call(f32[1]{0:T(128)S(6)} %copy.11.far_sigma.refs_0_, f32[3,4096]{1,0:T(4,128)} %refs_1_.1, f32[3,4096]{1,0:T(4,128)} %refs_2_.1, f32[3,2048]{1,0:T(4,128)} %refs_3_.1, s32[1,4096]{1,0:T(1,128)} %bitcast.2, bf16[64,4096]{1,0:T(8,128)(2,1)} %refs_5_.1, bf16[64,4096]{1,0:T(8,128)(2,1)} %collective-permute-done.refs_6_, ...), custom_call_target="tpu_custom_call" | custom-call | flops 11500000256 | tf_op jit(solution)/shard_map/score/pallas_call | solution.py:523
  22.5 1.5 %collective-permute-start.2 = (f32[88,128]{1,0:T(8,128)}, f32[88,128]{1,0:T(8,128)S(1)}, u32[]{:S(2)}, u32[]{:S(2)}) collective-permute-start(f32[88,128]{1,0:T(8,128)} %score.1.refs_0_), channel_id=1, source_target_pairs={{2,0},{0,2},{3,1},{1,3},{6,4},{4,6},{7,5},{5,7},{10,8},{8,10},{11,... | collective-permute-start | bytes 135176 | tf_op jit(solution)/shard_map/ppermute | solution.py:477
  24.1 0.0 collective-permute-done.5.refs_3_
  24.1 0.0 collective-permute-done.4.refs_2_
  24.1 1.3 %neighbours.1 = (s32[4,8,24,128]{3,2,1,0:T(8,128)S(1)}, s32[4,8,24,128]{3,2,1,0:T(8,128)S(1)}, f32[4,8,24,128]{3,2,1,0:T(8,128)S(1)}) custom-call(bf16[240,128]{1,0:T(8,128)(2,1)S(1)} %copy-done, bf16[240,128]{1,0:T(8,128)(2,1)S(1)} %collective-permute-done.3.refs_1_, bf16[240,128]{1,0:T(8,128)(2,1)S(1)} %collective-permute-done.4.refs_2_, ...), custom_call_target="tpu_custom_call" | custom-call | flops 2300000000 | tf_op jit(solution)/shard_map/neighbours/pallas_call | solution.py:546
  25.4 1.4 %collective-permute-done.2.refs_1_ = f32[88,128]{1,0:T(8,128)S(1)} collective-permute-done((f32[88,128]{1,0:T(8,128)}, f32[88,128]{1,0:T(8,128)S(1)}, u32[]{:S(2)}, u32[]{:S(2)}) %collective-permute-start.2) | collective-permute-done | bytes 45088 | tf_op jit(solution)/shard_map/ppermute | solution.py:477
  26.9 0.9 %collective-permute-start.8 = (f32[72,128]{1,0:T(8,128)S(1)}, f32[72,128]{1,0:T(8,128)S(1)}, u32[]{:S(2)}, u32[]{:S(2)}) collective-permute-start(f32[72,128]{1,0:T(8,128)S(1)} %get-tuple-element.15.refs_0_), channel_id=1, source_target_pairs={{12,0},{0,4},{4,8},{8,12},{13,1},{1,5},{5,9},{9,13},{14,2},{2,6},{... | collective-permute-start | bytes 110600 | tf_op jit(solution)/shard_map/ppermute | solution.py:477
  27.8 0.3 collective-permute-start.7
  28.2 2.8 %collective-permute-start.6 = (f32[72,128]{1,0:T(8,128)S(1)}, f32[72,128]{1,0:T(8,128)S(1)}, u32[]{:S(2)}, u32[]{:S(2)}) collective-permute-start(f32[72,128]{1,0:T(8,128)S(1)} %get-tuple-element.15.refs_0_), channel_id=1, source_target_pairs={{4,0},{8,4},{12,8},{0,12},{5,1},{9,5},{13,9},{1,13},{6,2},{10,6},{... | collective-permute-start | bytes 110600 | tf_op jit(solution)/shard_map/ppermute | solution.py:477
  31.0 2.0 %collective-permute-done.8.refs_3_ = f32[72,128]{1,0:T(8,128)S(1)} collective-permute-done((f32[72,128]{1,0:T(8,128)S(1)}, f32[72,128]{1,0:T(8,128)S(1)}, u32[]{:S(2)}, u32[]{:S(2)}) %collective-permute-start.8) | collective-permute-done | bytes 36896 | tf_op jit(solution)/shard_map/ppermute | solution.py:477
  33.0 0.5 %collective-permute-done.7.refs_2_ = f32[72,128]{1,0:T(8,128)S(1)} collective-permute-done((f32[72,128]{1,0:T(8,128)S(1)}, f32[72,128]{1,0:T(8,128)S(1)}, u32[]{:S(2)}, u32[]{:S(2)}) %collective-permute-start.7) | collective-permute-done | bytes 36896 | tf_op jit(solution)/shard_map/ppermute | solution.py:477
  33.5 0.0 collective-permute-done.6.refs_1_
  33.6 4.6 %sweeps.1.part = f32[3,2048]{1,0:T(4,128)S(1)} custom-call(f32[72,128]{1,0:T(8,128)S(1)} %get-tuple-element.15.refs_0_, f32[72,128]{1,0:T(8,128)S(1)} %collective-permute-done.6.refs_1_, f32[72,128]{1,0:T(8,128)S(1)} %collective-permute-done.7.refs_2_, f32[72,128]{1,0:T(8,128)S(1)} %collective-permute-done.8.refs_3_, ...), custom_call_target="tpu_custom_call" | custom-call | flops 8049999872 | tf_op jit(solution)/shard_map/sweeps/pallas_call | solution.py:585
  38.1 0.1 collective-permute-start.9
  38.2 0.5 %collective-permute-start.10 = (f32[17,128]{1,0:T(8,128)S(1)}, f32[17,128]{1,0:T(8,128)S(1)}, u32[]{:S(2)}, u32[]{:S(2)}) collective-permute-start(f32[17,128]{1,0:T(8,128)S(1)} %get-tuple-element.19.mass), channel_id=1, source_target_pairs={{1,0},{0,1},{3,2},{2,3},{5,4},{4,5},{7,6},{6,7},{9,8},{8,9},{11,10... | collective-permute-start | bytes 26120 | tf_op jit(solution)/shard_map/ppermute | solution.py:477
  38.7 0.8 %collective-permute-done.10.mass_far = f32[17,128]{1,0:T(8,128)S(1)} collective-permute-done((f32[17,128]{1,0:T(8,128)S(1)}, f32[17,128]{1,0:T(8,128)S(1)}, u32[]{:S(2)}, u32[]{:S(2)}) %collective-permute-start.10) | collective-permute-done | bytes 8736 | tf_op jit(solution)/shard_map/ppermute | solution.py:477
  39.5 0.6 %whole.1 = (f32[3,4096]{1,0:T(4,128)}, f32[32,128]{1,0:T(8,128)}) custom-call(f32[3,2048]{1,0:T(4,128)S(1)} %sweeps.1.part, f32[3,2048]{1,0:T(4,128)S(1)} %collective-permute-done.9.part_far, f32[17,128]{1,0:T(8,128)S(1)} %get-tuple-element.19.mass, f32[17,128]{1,0:T(8,128)S(1)} %collective-permute-done.10.mass_far), custom_call_target="tpu_custom_call" | custom-call | flops 575000000 | tf_op jit(solution)/shard_map/whole/pallas_call | solution.py:602
  (12 shorter events, 0.1 us)
Async XLA Ops:
  0.6 10.7 %collective-permute-start = (bf16[64,4096]{1,0:T(8,128)(2,1)}, bf16[64,4096]{1,0:T(8,128)(2,1)}, u32[]{:S(2)}, u32[]{:S(2)}) collective-permute-start(bf16[64,4096]{1,0:T(8,128)(2,1)} %refs_5_.1), channel_id=1, source_target_pairs={{1,0},{0,1},{3,2},{2,3},{5,4},{4,5},{7,6},{6,7},{9,8},{8,9},{11,10... | collective-permute-start | bytes 1572872 | tf_op jit(solution)/shard_map/ppermute | solution.py:477
  1.1 10.2 %collective-permute-start.1 = (bf16[64,2048]{1,0:T(8,128)(2,1)}, bf16[64,2048]{1,0:T(8,128)(2,1)}, u32[]{:S(2)}, u32[]{:S(2)}) collective-permute-start(bf16[64,2048]{1,0:T(8,128)(2,1)} %refs_7_.1), channel_id=1, source_target_pairs={{1,0},{0,1},{3,2},{2,3},{5,4},{4,5},{7,6},{6,7},{9,8},{8,9},{11,10... | collective-permute-start | bytes 786440 | tf_op jit(solution)/shard_map/ppermute | solution.py:477
  4.3 19.8 %collective-permute-start.5 = (bf16[240,128]{1,0:T(8,128)(2,1)}, bf16[240,128]{1,0:T(8,128)(2,1)S(1)}, u32[]{:S(2)}, u32[]{:S(2)}) collective-permute-start(bf16[240,128]{1,0:T(8,128)(2,1)} %get-tuple-element.13.refs_0_), channel_id=1, source_target_pairs={{12,0},{0,4},{4,8},{8,12},{13,1},{1,5},{5,9},{9,13},{14,2},{2,6},{... | collective-permute-start | bytes 184328 | tf_op jit(solution)/shard_map/ppermute | solution.py:477
  7.4 16.7 %collective-permute-start.4 = (bf16[240,128]{1,0:T(8,128)(2,1)}, bf16[240,128]{1,0:T(8,128)(2,1)S(1)}, u32[]{:S(2)}, u32[]{:S(2)}) collective-permute-start(bf16[240,128]{1,0:T(8,128)(2,1)} %get-tuple-element.13.refs_0_), channel_id=1, source_target_pairs={{8,0},{12,4},{0,8},{4,12},{9,1},{13,5},{1,9},{5,13},{10,2},{14,6},... | collective-permute-start | bytes 184328 | tf_op jit(solution)/shard_map/ppermute | solution.py:477
  10.0 14.1 %collective-permute-start.3 = (bf16[240,128]{1,0:T(8,128)(2,1)}, bf16[240,128]{1,0:T(8,128)(2,1)S(1)}, u32[]{:S(2)}, u32[]{:S(2)}) collective-permute-start(bf16[240,128]{1,0:T(8,128)(2,1)} %get-tuple-element.13.refs_0_), channel_id=1, source_target_pairs={{4,0},{8,4},{12,8},{0,12},{5,1},{9,5},{13,9},{1,13},{6,2},{10,6},{... | collective-permute-start | bytes 184328 | tf_op jit(solution)/shard_map/ppermute | solution.py:477
  11.3 12.8 %copy-start = (bf16[240,128]{1,0:T(8,128)(2,1)S(1)}, bf16[240,128]{1,0:T(8,128)(2,1)}, u32[]{:S(2)}) copy-start(bf16[240,128]{1,0:T(8,128)(2,1)} %get-tuple-element.13.refs_0_) | copy-start | bytes 184324
  22.5 4.3 %copy-start.1 = (f32[88,128]{1,0:T(8,128)S(1)}, f32[88,128]{1,0:T(8,128)}, u32[]{:S(2)}) copy-start(f32[88,128]{1,0:T(8,128)} %score.1.refs_0_) | copy-start | bytes 135172
  22.5 4.3 %copy-start.2 = (f32[5,17,128]{2,1,0:T(8,128)S(1)}, f32[5,17,128]{2,1,0:T(8,128)}, u32[]{:S(2)}) copy-start(f32[5,17,128]{2,1,0:T(8,128)} %get-tuple-element.12.z_ref) | copy-start | bytes 130564
  22.5 4.3 %collective-permute-start.2 = (f32[88,128]{1,0:T(8,128)}, f32[88,128]{1,0:T(8,128)S(1)}, u32[]{:S(2)}, u32[]{:S(2)}) collective-permute-start(f32[88,128]{1,0:T(8,128)} %score.1.refs_0_), channel_id=1, source_target_pairs={{2,0},{0,2},{3,1},{1,3},{6,4},{4,6},{7,5},{5,7},{10,8},{8,10},{11,... | collective-permute-start | bytes 135176 | tf_op jit(solution)/shard_map/ppermute | solution.py:477
  26.9 6.7 %copy-start.3 = (f32[4,17,128]{2,1,0:T(8,128)S(1)}, f32[4,17,128]{2,1,0:T(8,128)}, u32[]{:S(2)}) copy-start(f32[4,17,128]{2,1,0:T(8,128)} %get-tuple-element.18.refs_7_) | copy-start | bytes 104452
  26.9 6.1 %collective-permute-start.8 = (f32[72,128]{1,0:T(8,128)S(1)}, f32[72,128]{1,0:T(8,128)S(1)}, u32[]{:S(2)}, u32[]{:S(2)}) collective-permute-start(f32[72,128]{1,0:T(8,128)S(1)} %get-tuple-element.15.refs_0_), channel_id=1, source_target_pairs={{12,0},{0,4},{4,8},{8,12},{13,1},{1,5},{5,9},{9,13},{14,2},{2,6},{... | collective-permute-start | bytes 110600 | tf_op jit(solution)/shard_map/ppermute | solution.py:477
  27.8 5.7 %collective-permute-start.7 = (f32[72,128]{1,0:T(8,128)S(1)}, f32[72,128]{1,0:T(8,128)S(1)}, u32[]{:S(2)}, u32[]{:S(2)}) collective-permute-start(f32[72,128]{1,0:T(8,128)S(1)} %get-tuple-element.15.refs_0_), channel_id=1, source_target_pairs={{8,0},{12,4},{0,8},{4,12},{9,1},{13,5},{1,9},{5,13},{10,2},{14,6},... | collective-permute-start | bytes 110600 | tf_op jit(solution)/shard_map/ppermute | solution.py:477
  28.2 5.4 %collective-permute-start.6 = (f32[72,128]{1,0:T(8,128)S(1)}, f32[72,128]{1,0:T(8,128)S(1)}, u32[]{:S(2)}, u32[]{:S(2)}) collective-permute-start(f32[72,128]{1,0:T(8,128)S(1)} %get-tuple-element.15.refs_0_), channel_id=1, source_target_pairs={{4,0},{8,4},{12,8},{0,12},{5,1},{9,5},{13,9},{1,13},{6,2},{10,6},{... | collective-permute-start | bytes 110600 | tf_op jit(solution)/shard_map/ppermute | solution.py:477
  38.1 1.4 %collective-permute-start.9 = (f32[3,2048]{1,0:T(4,128)S(1)}, f32[3,2048]{1,0:T(4,128)S(1)}, u32[]{:S(2)}, u32[]{:S(2)}) collective-permute-start(f32[3,2048]{1,0:T(4,128)S(1)} %sweeps.1.part), channel_id=1, source_target_pairs={{1,0},{0,1},{3,2},{2,3},{5,4},{4,5},{7,6},{6,7},{9,8},{8,9},{11,10... | collective-permute-start | bytes 73736 | tf_op jit(solution)/shard_map/ppermute | solution.py:477
  38.2 1.3 %collective-permute-start.10 = (f32[17,128]{1,0:T(8,128)S(1)}, f32[17,128]{1,0:T(8,128)S(1)}, u32[]{:S(2)}, u32[]{:S(2)}) collective-permute-start(f32[17,128]{1,0:T(8,128)S(1)} %get-tuple-element.19.mass), channel_id=1, source_target_pairs={{1,0},{0,1},{3,2},{2,3},{5,4},{4,5},{7,6},{6,7},{9,8},{8,9},{11,10... | collective-permute-start | bytes 26120 | tf_op jit(solution)/shard_map/ppermute | solution.py:477

commit v2 on v1

--- a/solution.py
+++ b/solution.py
@@ -96,8 +96,8 @@
 
 
 def score_kernel(*refs, chunk, tile):
-    far, state, near = refs[:9], refs[9], refs[10:19]
-    cols, aug, x_cols, left, score, highest, done = refs[19:]
+    far, state, near = refs[:9], refs[10], refs[11:20]
+    cols, aug, x_cols, left, score, highest, done = refs[20:]
     slots = far[1].shape[1]
     points = cols.shape[0]
     mine = pl.ds(pl.multiple_of(first_slot(slots), LANES), points)
@@ -208,32 +208,41 @@
     return first_slot(slots) + LANES * rows + lane_ids(blocks)
 
 
-def merge_kernel(z_ref, *refs):
-    *states, _, terms, mass_out = refs
+def own_kernel(state, z_ref, geo, out, geo_out):
+    geo_out[...] = geo[...]
     blocks = z_ref.shape[1]
-    live = z_ref[3]
+    for q in range(5):
+        out[q] = state[q * blocks : (q + 1) * blocks, :]
+    z = [z_ref[c] for c in range(3)]
     sigma = z_ref[4]
-
-    def part(ref, q):
-        return ref[q * blocks : (q + 1) * blocks, :]
-
-    peak = part(states[0], 4)
-    for ref in states[1:]:
-        peak = jnp.maximum(peak, part(ref, 4))
+    for c in range(3):
+        out[5 + c] = z[c]
+    norm = (z[0] * z[0] + z[1] * z[1] + z[2] * z[2]) * (0.5 / sigma)
+    out[8] = (norm + outlier_level) * LOG2E
+    out[9] = z_ref[3]
+    out[10] = sigma
+
+
+def merge_kernel(own, *refs):
+    *others, terms, mass_out = refs
+    blocks = own.shape[1]
+    states = [[own[q] for q in range(5)]]
+    for ref in others:
+        states.append([ref[q * blocks : (q + 1) * blocks, :] for q in range(5)])
+    peak = states[0][4]
+    for state in states[1:]:
+        peak = jnp.maximum(peak, state[4])
     sums = [jnp.zeros((blocks, LANES), F32)] * 4
-    for ref in states:
-        factor = jnp.exp2(part(ref, 4) - peak)
-        sums = [s + part(ref, q) * factor for q, s in enumerate(sums)]
-    z = [z_ref[c] for c in range(3)]
-    norm = (z[0] * z[0] + z[1] * z[1] + z[2] * z[2]) * (0.5 / sigma)
-    denom = sums[3] + jnp.exp2((norm + outlier_level) * LOG2E - peak)
-    each = live / denom
+    for state in states:
+        factor = jnp.exp2(state[4] - peak)
+        sums = [s + state[q] * factor for q, s in enumerate(sums)]
+    denom = sums[3] + jnp.exp2(own[8] - peak)
+    each = own[9] / denom
     mass = sums[3] * each
-    diag = mass + coherence * sigma
-    inverse = 1.0 / diag
+    inverse = 1.0 / (mass + coherence * own[10])
     terms[...] = jnp.zeros_like(terms)
     for c in range(3):
-        terms[c * blocks : (c + 1) * blocks, :] = (sums[c] * each - mass * z[c]) * inverse
+        terms[c * blocks : (c + 1) * blocks, :] = (sums[c] * each - mass * own[5 + c]) * inverse
     terms[3 * blocks : 4 * blocks, :] = mass * inverse
     mass_out[...] = mass
 
@@ -307,7 +316,7 @@
 
     for d in range(strips):
         wide[...] = geos[d][...].astype(F32)
-        j = lax.rem(lax.axis_index("strip") + d, strips)
+        j = lax.rem(lax.axis_index("strip") + strips - d, strips)
 
         for k in range(EDGES):
             fill_rows(rows, wide[k * blocks : (k + 1) * blocks, :])
@@ -369,7 +378,7 @@
     field[strips + 1] = jnp.zeros_like(field[0])
 
     for d in range(strips):
-        j = lax.rem(lax.axis_index("strip") + d, strips)
+        j = lax.rem(lax.axis_index("strip") + strips - d, strips)
         for q in range(4):
             fill_rows(rows, terms[d][q * blocks : (q + 1) * blocks, :])
 
@@ -474,7 +483,7 @@
 def around(array, axis):
     count = lax.axis_size(axis)
     return [array] + [
-        lax.ppermute(array, axis, [((i + d) % count, i) for i in range(count)]) for d in range(1, count)
+        lax.ppermute(array, axis, [(i, (i + d) % count) for i in range(count)]) for d in range(1, count)
     ]
 
 
@@ -512,8 +521,6 @@
         compiler_params=pltpu.CompilerParams(vmem_limit_bytes=(64 << 20) - (64 << 10)),
         cost_estimate=takes(2),
     )(*own, counts, sigma_sq)
-    geos = around(geo, "strip")
-
     arrays = (src_pos, displacement, tgt_pos, seed_target.reshape(1, slots))
     features = (src_feat, src_other, tgt_feat, tgt_other)
     tile = 256
@@ -524,7 +531,7 @@
         functools.partial(score_kernel, chunk=points // 8, tile=tile),
         name="score",
         out_shape=jax.ShapeDtypeStruct((state_rows, LANES), F32),
-        in_specs=[hbm] * 9,
+        in_specs=[hbm] * 9 + [pl.BlockSpec(memory_space=pl.ANY)],
         out_specs=VMEM,
         scratch_shapes=scalars[1:]
         + [pltpu.VMEM(array.shape, array.dtype) for array in arrays]
@@ -540,8 +547,21 @@
         ],
         compiler_params=pltpu.CompilerParams(vmem_limit_bytes=60 << 20),
         cost_estimate=takes(10),
-    )(sigma_sq, *arrays, *features)
-
+    )(sigma_sq, *arrays, *features, z)
+
+    own, geo = pl.pallas_call(
+        own_kernel,
+        name="own",
+        out_shape=(
+            jax.ShapeDtypeStruct((11, blocks, LANES), F32),
+            jax.ShapeDtypeStruct((geo_rows, LANES), BF16),
+        ),
+        in_specs=[VMEM] * 3,
+        out_specs=(VMEM, VMEM),
+        compiler_params=small,
+        cost_estimate=takes(0.5),
+    )(state, z, geo)
+    geos = around(geo, "strip")
     shape = (strips, EDGES, ROWS_WIN, LANES)
     index, segment, weight = pl.pallas_call(
         functools.partial(kernels_kernel, strips=strips, blocks=blocks),
@@ -573,11 +593,11 @@
             jax.ShapeDtypeStruct((term_rows, LANES), F32),
             jax.ShapeDtypeStruct((blocks, LANES), F32),
         ),
-        in_specs=[VMEM] * (1 + len(states)) + [pl.BlockSpec(memory_space=pl.ANY)],
+        in_specs=[VMEM] * len(states),
         out_specs=(VMEM, VMEM),
         compiler_params=small,
         cost_estimate=takes(0.5),
-    )(z, *states, weight)
+    )(own, *states[1:])
 
     all_terms = around(terms, "strip")
     mass_far = around(mass, "feat")[1]

time: 40.4 us -> 38.6 us (0.955)
  waiting for transfers between devices: 4.85 us -> 2.37 us
  local copies, waits for them, and re-layouts: 0.02 us -> 0.83 us
    ppermute x11, waiting for transfers between devices: 4.85 us -> 2.37 us  [around(): lax.ppermute(array, axis, [(i, (i + d) % count) for i in range(count)])]
    unnamed x8, local copies, waits for them, and re-layouts: 0.02 us -> 0.83 us
  transfers between devices with their start and end apart: 11 -> 11, of which waited for: 4 -> 3; matrix products, arithmetic and copies ran while one was open for 0% -> 0% of each run, Pallas kernels for 36% -> 8%
where the time goes in v2:
time: 38.6 us; the launch traced here: 38.4 us
  Pallas kernels  19.6 us (51%)
  starting transfers between devices  13.6 us (35%)
  waiting for transfers between devices  2.37 us (6%)
  between operations  2.02 us (5%)
  local copies, waits for them, and re-layouts  0.83 us (2%)
    ppermute x11, starting transfers between devices, around(): lax.ppermute(array, axis, [(i, (i + d) % count) for i in range(count)])  13.6 us
    pallas_call x1, Pallas kernels, on_device(): pl.pallas_call(functools.partial(score_kernel, chunk=points // 8, tile=ti...  11.2 us
    pallas_call x1, Pallas kernels, on_device(): pl.pallas_call(functools.partial(sweep_kernel, strips=strips, blocks=bloc...  4.55 us
    ppermute x11, waiting for transfers between devices, around(): lax.ppermute(array, axis, [(i, (i + d) % count) for i in range(count)])  2.37 us
    pallas_call x1, Pallas kernels, on_device(): pl.pallas_call(geometry_kernel, name='geometry', out_shape=(jax.ShapeDtyp...  1.81 us
    pallas_call x1, Pallas kernels, on_device(): pl.pallas_call(functools.partial(kernels_kernel, strips=strips, blocks=bl...  1.31 us
    unnamed x8, local copies, waits for them, and re-layouts  0.83 us
  transfers between devices with their start and end apart: 11, of which 3 were waited for; matrix products, arithmetic and copies ran while one was open for 0% of the time, Pallas kernels for 8%

profile of v2, /device:TPU:0, one launch (start us, length us, event | category | flops | bytes accessed | tf_op | source)
XLA Modules:
  0.0 38.4 jit_solution(188615912249860742)
XLA Ops:
  0.6 0.5 %collective-permute-start = (bf16[64,4096]{1,0:T(8,128)(2,1)}, bf16[64,4096]{1,0:T(8,128)(2,1)}, u32[]{:S(2)}, u32[]{:S(2)}) collective-permute-start(bf16[64,4096]{1,0:T(8,128)(2,1)} %refs_5_.1), channel_id=1, source_target_pairs={{0,1},{1,0},{2,3},{3,2},{4,5},{5,4},{6,7},{7,6},{8,9},{9,8},{10,11... | collective-permute-start | bytes 1572872 | tf_op jit(solution)/shard_map/ppermute | solution.py:486
  1.1 0.1 collective-permute-start.1
  2.5 1.8 %geometry.1 = (bf16[240,128]{1,0:T(8,128)(2,1)}, f32[5,17,128]{2,1,0:T(8,128)}, f32[4,17,128]{2,1,0:T(8,128)}) custom-call(f32[3,4096]{1,0:T(4,128)} %refs_1_.1, f32[3,4096]{1,0:T(4,128)} %refs_2_.1, s32[8,4096]{1,0:T(8,128)} %far_edges.1, s32[1]{0:T(128)S(6)} %copy.12.far_counts, f32[1]{0:T(128)S(6)} %copy.11.far_sigma.refs_0_), custom_call_target="tpu_custom_call" | custom-call | flops 2300000000 | tf_op jit(solution)/shard_map/geometry/pallas_call | solution.py:508
  4.3 0.0 collective-permute-done.1.refs_8_
  4.4 0.0 collective-permute-done.refs_6_
  4.4 0.0 copy-start.1
  4.4 11.2 %score.1.state = f32[88,128]{1,0:T(8,128)} custom-call(f32[1]{0:T(128)S(6)} %copy.11.far_sigma.refs_0_, f32[3,4096]{1,0:T(4,128)} %refs_1_.1, f32[3,4096]{1,0:T(4,128)} %refs_2_.1, f32[3,2048]{1,0:T(4,128)} %refs_3_.1, s32[1,4096]{1,0:T(1,128)} %bitcast.2, bf16[64,4096]{1,0:T(8,128)(2,1)} %refs_5_.1, bf16[64,4096]{1,0:T(8,128)(2,1)} %collective-permute-done.refs_6_, ...), custom_call_target="tpu_custom_call" | custom-call | flops 11500000256 | tf_op jit(solution)/shard_map/score/pallas_call | solution.py:530
  15.6 3.0 %collective-permute-start.2 = (f32[88,128]{1,0:T(8,128)}, f32[88,128]{1,0:T(8,128)S(1)}, u32[]{:S(2)}, u32[]{:S(2)}) collective-permute-start(f32[88,128]{1,0:T(8,128)} %score.1.state), channel_id=1, source_target_pairs={{0,2},{2,0},{1,3},{3,1},{4,6},{6,4},{5,7},{7,5},{8,10},{10,8},{9,1... | collective-permute-start | bytes 135176 | tf_op jit(solution)/shard_map/ppermute | solution.py:486
  18.6 0.8 %copy-done = f32[88,128]{1,0:T(8,128)S(1)} copy-done((f32[88,128]{1,0:T(8,128)S(1)}, f32[88,128]{1,0:T(8,128)}, u32[]{:S(2)}) %copy-start) | copy-done | bytes 45080
  19.4 1.6 %collective-permute-start.6 = (bf16[240,128]{1,0:T(8,128)(2,1)S(1)}, bf16[240,128]{1,0:T(8,128)(2,1)S(1)}, u32[]{:S(2)}, u32[]{:S(2)}) collective-permute-start(bf16[240,128]{1,0:T(8,128)(2,1)S(1)} %get-tuple-element.18.refs_0_), channel_id=1, source_target_pairs={{0,4},{4,8},{8,12},{12,0},{1,5},{5,9},{9,13},{13,1},{2,6},{6,10},{... | collective-permute-start | bytes 184328 | tf_op jit(solution)/shard_map/ppermute | solution.py:486
  21.0 2.6 %collective-permute-start.7 = (bf16[240,128]{1,0:T(8,128)(2,1)S(1)}, bf16[240,128]{1,0:T(8,128)(2,1)S(1)}, u32[]{:S(2)}, u32[]{:S(2)}) collective-permute-start(bf16[240,128]{1,0:T(8,128)(2,1)S(1)} %get-tuple-element.18.refs_0_), channel_id=1, source_target_pairs={{0,8},{4,12},{8,0},{12,4},{1,9},{5,13},{9,1},{13,5},{2,10},{6,14},... | collective-permute-start | bytes 184328 | tf_op jit(solution)/shard_map/ppermute | solution.py:486
  23.6 1.4 %collective-permute-start.8 = (bf16[240,128]{1,0:T(8,128)(2,1)S(1)}, bf16[240,128]{1,0:T(8,128)(2,1)S(1)}, u32[]{:S(2)}, u32[]{:S(2)}) collective-permute-start(bf16[240,128]{1,0:T(8,128)(2,1)S(1)} %get-tuple-element.18.refs_0_), channel_id=1, source_target_pairs={{0,12},{4,0},{8,4},{12,8},{1,13},{5,1},{9,5},{13,9},{2,14},{6,2},{... | collective-permute-start | bytes 184328 | tf_op jit(solution)/shard_map/ppermute | solution.py:486
  25.0 0.0 collective-permute-done.2.refs_0_
  25.0 0.7 %collective-permute-start.3 = (f32[72,128]{1,0:T(8,128)S(1)}, f32[72,128]{1,0:T(8,128)S(1)}, u32[]{:S(2)}, u32[]{:S(2)}) collective-permute-start(f32[72,128]{1,0:T(8,128)S(1)} %get-tuple-element.17.refs_0_), channel_id=1, source_target_pairs={{0,4},{4,8},{8,12},{12,0},{1,5},{5,9},{9,13},{13,1},{2,6},{6,10},{... | collective-permute-start | bytes 110600 | tf_op jit(solution)/shard_map/ppermute | solution.py:486
  25.8 0.3 collective-permute-start.4
  26.1 2.8 %collective-permute-start.5 = (f32[72,128]{1,0:T(8,128)S(1)}, f32[72,128]{1,0:T(8,128)S(1)}, u32[]{:S(2)}, u32[]{:S(2)}) collective-permute-start(f32[72,128]{1,0:T(8,128)S(1)} %get-tuple-element.17.refs_0_), channel_id=1, source_target_pairs={{0,12},{4,0},{8,4},{12,8},{1,13},{5,1},{9,5},{13,9},{2,14},{6,2},{... | collective-permute-start | bytes 110600 | tf_op jit(solution)/shard_map/ppermute | solution.py:486
  28.9 1.3 %neighbours.1 = (s32[4,8,24,128]{3,2,1,0:T(8,128)S(1)}, s32[4,8,24,128]{3,2,1,0:T(8,128)S(1)}, f32[4,8,24,128]{3,2,1,0:T(8,128)S(1)}) custom-call(bf16[240,128]{1,0:T(8,128)(2,1)S(1)} %get-tuple-element.18.refs_0_, bf16[240,128]{1,0:T(8,128)(2,1)S(1)} %collective-permute-done.6.refs_1_, bf16[240,128]{1,0:T(8,128)(2,1)S(1)} %collective-permute-done.7.refs_2_, ...), custom_call_target="tpu_custom_call" | custom-call | flops 2300000000 | tf_op jit(solution)/shard_map/neighbours/pallas_call | solution.py:566
  30.2 0.7 %collective-permute-done.3.refs_1_ = f32[72,128]{1,0:T(8,128)S(1)} collective-permute-done((f32[72,128]{1,0:T(8,128)S(1)}, f32[72,128]{1,0:T(8,128)S(1)}, u32[]{:S(2)}, u32[]{:S(2)}) %collective-permute-start.3) | collective-permute-done | bytes 36896 | tf_op jit(solution)/shard_map/ppermute | solution.py:486
  30.9 0.8 %collective-permute-done.4.refs_2_ = f32[72,128]{1,0:T(8,128)S(1)} collective-permute-done((f32[72,128]{1,0:T(8,128)S(1)}, f32[72,128]{1,0:T(8,128)S(1)}, u32[]{:S(2)}, u32[]{:S(2)}) %collective-permute-start.4) | collective-permute-done | bytes 36896 | tf_op jit(solution)/shard_map/ppermute | solution.py:486
  31.8 4.6 %sweeps.1.part = f32[3,2048]{1,0:T(4,128)S(1)} custom-call(f32[72,128]{1,0:T(8,128)S(1)} %get-tuple-element.17.refs_0_, f32[72,128]{1,0:T(8,128)S(1)} %collective-permute-done.3.refs_1_, f32[72,128]{1,0:T(8,128)S(1)} %collective-permute-done.4.refs_2_, f32[72,128]{1,0:T(8,128)S(1)} %collective-permute-done.5.refs_3_, ...), custom_call_target="tpu_custom_call" | custom-call | flops 8049999872 | tf_op jit(solution)/shard_map/sweeps/pallas_call | solution.py:605
  36.3 0.1 collective-permute-start.9
  36.4 0.5 %collective-permute-start.10 = (f32[17,128]{1,0:T(8,128)S(1)}, f32[17,128]{1,0:T(8,128)S(1)}, u32[]{:S(2)}, u32[]{:S(2)}) collective-permute-start(f32[17,128]{1,0:T(8,128)S(1)} %get-tuple-element.23.mass), channel_id=1, source_target_pairs={{0,1},{1,0},{2,3},{3,2},{4,5},{5,4},{6,7},{7,6},{8,9},{9,8},{10,11... | collective-permute-start | bytes 26120 | tf_op jit(solution)/shard_map/ppermute | solution.py:486
  36.9 0.8 %collective-permute-done.10.mass_far = f32[17,128]{1,0:T(8,128)S(1)} collective-permute-done((f32[17,128]{1,0:T(8,128)S(1)}, f32[17,128]{1,0:T(8,128)S(1)}, u32[]{:S(2)}, u32[]{:S(2)}) %collective-permute-start.10) | collective-permute-done | bytes 8736 | tf_op jit(solution)/shard_map/ppermute | solution.py:486
  37.7 0.6 %whole.1 = (f32[3,4096]{1,0:T(4,128)}, f32[32,128]{1,0:T(8,128)}) custom-call(f32[3,2048]{1,0:T(4,128)S(1)} %sweeps.1.part, f32[3,2048]{1,0:T(4,128)S(1)} %collective-permute-done.9.part_far, f32[17,128]{1,0:T(8,128)S(1)} %get-tuple-element.23.mass, f32[17,128]{1,0:T(8,128)S(1)} %collective-permute-done.10.mass_far), custom_call_target="tpu_custom_call" | custom-call | flops 575000000 | tf_op jit(solution)/shard_map/whole/pallas_call | solution.py:622
  (13 shorter events, 0.1 us)
Async XLA Ops:
  0.6 3.7 %collective-permute-start = (bf16[64,4096]{1,0:T(8,128)(2,1)}, bf16[64,4096]{1,0:T(8,128)(2,1)}, u32[]{:S(2)}, u32[]{:S(2)}) collective-permute-start(bf16[64,4096]{1,0:T(8,128)(2,1)} %refs_5_.1), channel_id=1, source_target_pairs={{0,1},{1,0},{2,3},{3,2},{4,5},{5,4},{6,7},{7,6},{8,9},{9,8},{10,11... | collective-permute-start | bytes 1572872 | tf_op jit(solution)/shard_map/ppermute | solution.py:486
  1.1 3.2 %collective-permute-start.1 = (bf16[64,2048]{1,0:T(8,128)(2,1)}, bf16[64,2048]{1,0:T(8,128)(2,1)}, u32[]{:S(2)}, u32[]{:S(2)}) collective-permute-start(bf16[64,2048]{1,0:T(8,128)(2,1)} %refs_7_.1), channel_id=1, source_target_pairs={{0,1},{1,0},{2,3},{3,2},{4,5},{5,4},{6,7},{7,6},{8,9},{9,8},{10,11... | collective-permute-start | bytes 786440 | tf_op jit(solution)/shard_map/ppermute | solution.py:486
  4.4 14.2 %copy-start.1 = (bf16[240,128]{1,0:T(8,128)(2,1)S(1)}, bf16[240,128]{1,0:T(8,128)(2,1)}, u32[]{:S(2)}) copy-start(bf16[240,128]{1,0:T(8,128)(2,1)} %get-tuple-element.15.geo) | copy-start | bytes 184324
  4.4 14.2 %copy-start.2 = (f32[5,17,128]{2,1,0:T(8,128)S(1)}, f32[5,17,128]{2,1,0:T(8,128)}, u32[]{:S(2)}) copy-start(f32[5,17,128]{2,1,0:T(8,128)} %get-tuple-element.14.refs_9_.z_ref) | copy-start | bytes 130564
  15.6 9.4 %collective-permute-start.2 = (f32[88,128]{1,0:T(8,128)}, f32[88,128]{1,0:T(8,128)S(1)}, u32[]{:S(2)}, u32[]{:S(2)}) collective-permute-start(f32[88,128]{1,0:T(8,128)} %score.1.state), channel_id=1, source_target_pairs={{0,2},{2,0},{1,3},{3,1},{4,6},{6,4},{5,7},{7,5},{8,10},{10,8},{9,1... | collective-permute-start | bytes 135176 | tf_op jit(solution)/shard_map/ppermute | solution.py:486
  18.6 0.8 %copy-start = (f32[88,128]{1,0:T(8,128)S(1)}, f32[88,128]{1,0:T(8,128)}, u32[]{:S(2)}) copy-start(f32[88,128]{1,0:T(8,128)} %score.1.state) | copy-start | bytes 135172
  19.4 6.7 %collective-permute-start.6 = (bf16[240,128]{1,0:T(8,128)(2,1)S(1)}, bf16[240,128]{1,0:T(8,128)(2,1)S(1)}, u32[]{:S(2)}, u32[]{:S(2)}) collective-permute-start(bf16[240,128]{1,0:T(8,128)(2,1)S(1)} %get-tuple-element.18.refs_0_), channel_id=1, source_target_pairs={{0,4},{4,8},{8,12},{12,0},{1,5},{5,9},{9,13},{13,1},{2,6},{6,10},{... | collective-permute-start | bytes 184328 | tf_op jit(solution)/shard_map/ppermute | solution.py:486
  21.0 7.9 %collective-permute-start.7 = (bf16[240,128]{1,0:T(8,128)(2,1)S(1)}, bf16[240,128]{1,0:T(8,128)(2,1)S(1)}, u32[]{:S(2)}, u32[]{:S(2)}) collective-permute-start(bf16[240,128]{1,0:T(8,128)(2,1)S(1)} %get-tuple-element.18.refs_0_), channel_id=1, source_target_pairs={{0,8},{4,12},{8,0},{12,4},{1,9},{5,13},{9,1},{13,5},{2,10},{6,14},... | collective-permute-start | bytes 184328 | tf_op jit(solution)/shard_map/ppermute | solution.py:486
  23.6 5.3 %collective-permute-start.8 = (bf16[240,128]{1,0:T(8,128)(2,1)S(1)}, bf16[240,128]{1,0:T(8,128)(2,1)S(1)}, u32[]{:S(2)}, u32[]{:S(2)}) collective-permute-start(bf16[240,128]{1,0:T(8,128)(2,1)S(1)} %get-tuple-element.18.refs_0_), channel_id=1, source_target_pairs={{0,12},{4,0},{8,4},{12,8},{1,13},{5,1},{9,5},{13,9},{2,14},{6,2},{... | collective-permute-start | bytes 184328 | tf_op jit(solution)/shard_map/ppermute | solution.py:486
  25.0 6.7 %copy-start.3 = (f32[4,17,128]{2,1,0:T(8,128)S(1)}, f32[4,17,128]{2,1,0:T(8,128)}, u32[]{:S(2)}) copy-start(f32[4,17,128]{2,1,0:T(8,128)} %get-tuple-element.22.refs_7_) | copy-start | bytes 104452
  25.0 5.9 %collective-permute-start.3 = (f32[72,128]{1,0:T(8,128)S(1)}, f32[72,128]{1,0:T(8,128)S(1)}, u32[]{:S(2)}, u32[]{:S(2)}) collective-permute-start(f32[72,128]{1,0:T(8,128)S(1)} %get-tuple-element.17.refs_0_), channel_id=1, source_target_pairs={{0,4},{4,8},{8,12},{12,0},{1,5},{5,9},{9,13},{13,1},{2,6},{6,10},{... | collective-permute-start | bytes 110600 | tf_op jit(solution)/shard_map/ppermute | solution.py:486
  25.8 6.0 %collective-permute-start.4 = (f32[72,128]{1,0:T(8,128)S(1)}, f32[72,128]{1,0:T(8,128)S(1)}, u32[]{:S(2)}, u32[]{:S(2)}) collective-permute-start(f32[72,128]{1,0:T(8,128)S(1)} %get-tuple-element.17.refs_0_), channel_id=1, source_target_pairs={{0,8},{4,12},{8,0},{12,4},{1,9},{5,13},{9,1},{13,5},{2,10},{6,14},... | collective-permute-start | bytes 110600 | tf_op jit(solution)/shard_map/ppermute | solution.py:486
  26.1 5.7 %collective-permute-start.5 = (f32[72,128]{1,0:T(8,128)S(1)}, f32[72,128]{1,0:T(8,128)S(1)}, u32[]{:S(2)}, u32[]{:S(2)}) collective-permute-start(f32[72,128]{1,0:T(8,128)S(1)} %get-tuple-element.17.refs_0_), channel_id=1, source_target_pairs={{0,12},{4,0},{8,4},{12,8},{1,13},{5,1},{9,5},{13,9},{2,14},{6,2},{... | collective-permute-start | bytes 110600 | tf_op jit(solution)/shard_map/ppermute | solution.py:486
  36.3 1.4 %collective-permute-start.9 = (f32[3,2048]{1,0:T(4,128)S(1)}, f32[3,2048]{1,0:T(4,128)S(1)}, u32[]{:S(2)}, u32[]{:S(2)}) collective-permute-start(f32[3,2048]{1,0:T(4,128)S(1)} %sweeps.1.part), channel_id=1, source_target_pairs={{0,1},{1,0},{2,3},{3,2},{4,5},{5,4},{6,7},{7,6},{8,9},{9,8},{10,11... | collective-permute-start | bytes 73736 | tf_op jit(solution)/shard_map/ppermute | solution.py:486
  36.4 1.3 %collective-permute-start.10 = (f32[17,128]{1,0:T(8,128)S(1)}, f32[17,128]{1,0:T(8,128)S(1)}, u32[]{:S(2)}, u32[]{:S(2)}) collective-permute-start(f32[17,128]{1,0:T(8,128)S(1)} %get-tuple-element.23.mass), channel_id=1, source_target_pairs={{0,1},{1,0},{2,3},{3,2},{4,5},{5,4},{6,7},{7,6},{8,9},{9,8},{10,11... | collective-permute-start | bytes 26120 | tf_op jit(solution)/shard_map/ppermute | solution.py:486

commit v3 on v2

--- a/solution.py
+++ b/solution.py
@@ -189,11 +189,8 @@
         for t in range(tiles):
             shift = jnp.where(ids + float(t * tile) == seed, tied, peak)
             weight = jnp.exp2(score[t, r : r + chunk] * (feature_scale * LOG2E) - shift)
-            high = weight.astype(BF16)
-            low = (weight - high.astype(F32)).astype(BF16)
             x = x_cols[t * tile : (t + 1) * tile, :]
-            total += jnp.dot(high, x, preferred_element_type=F32)
-            total += jnp.dot(low, x, preferred_element_type=F32)
+            total += jnp.dot(weight.astype(BF16), x, preferred_element_type=F32)
         total = jnp.where(lane_ids() == 4, peak, total)
         highest[r : r + chunk] = total
     for at in range(blocks):

time: 38.6 us -> 36.5 us (0.946)
  Pallas kernels: 19.6 us -> 17.4 us
    pallas_call x1, Pallas kernels: 11.2 us -> 9.07 us  [on_device(): pl.pallas_call(functools.partial(score_kernel, chunk=points // 8, tile=ti...]
  transfers between devices with their start and end apart: 11 -> 11, of which waited for: 3 -> 3; matrix products, arithmetic and copies ran while one was open for 0% -> 0% of each run, Pallas kernels for 8% -> 9%
where the time goes in v3:
time: 36.5 us; the launch traced here: 36.2 us
  Pallas kernels  17.4 us (48%)
  starting transfers between devices  13.6 us (37%)
  waiting for transfers between devices  2.37 us (6%)
  between operations  2.02 us (6%)
  local copies, waits for them, and re-layouts  0.83 us (2%)
    ppermute x11, starting transfers between devices, around(): lax.ppermute(array, axis, [(i, (i + d) % count) for i in range(count)])  13.6 us
    pallas_call x1, Pallas kernels, on_device(): pl.pallas_call(functools.partial(score_kernel, chunk=points // 8, tile=ti...  9.07 us
    pallas_call x1, Pallas kernels, on_device(): pl.pallas_call(functools.partial(sweep_kernel, strips=strips, blocks=bloc...  4.55 us
    ppermute x11, waiting for transfers between devices, around(): lax.ppermute(array, axis, [(i, (i + d) % count) for i in range(count)])  2.37 us
    pallas_call x1, Pallas kernels, on_device(): pl.pallas_call(geometry_kernel, name='geometry', out_shape=(jax.ShapeDtyp...  1.81 us
    pallas_call x1, Pallas kernels, on_device(): pl.pallas_call(functools.partial(kernels_kernel, strips=strips, blocks=bl...  1.31 us
    unnamed x8, local copies, waits for them, and re-layouts  0.83 us
  transfers between devices with their start and end apart: 11, of which 3 were waited for; matrix products, arithmetic and copies ran while one was open for 0% of the time, Pallas kernels for 9%

profile of v3, /device:TPU:0, one launch (start us, length us, event | category | flops | bytes accessed | tf_op | source)
XLA Modules:
  0.0 36.2 jit_solution(18182652592744628039)
XLA Ops:
  0.6 0.5 %collective-permute-start = (bf16[64,4096]{1,0:T(8,128)(2,1)}, bf16[64,4096]{1,0:T(8,128)(2,1)}, u32[]{:S(2)}, u32[]{:S(2)}) collective-permute-start(bf16[64,4096]{1,0:T(8,128)(2,1)} %refs_5_.1), channel_id=1, source_target_pairs={{0,1},{1,0},{2,3},{3,2},{4,5},{5,4},{6,7},{7,6},{8,9},{9,8},{10,11... | collective-permute-start | bytes 1572872 | tf_op jit(solution)/shard_map/ppermute | solution.py:483
  1.1 0.1 collective-permute-start.1
  2.5 1.8 %geometry.1 = (bf16[240,128]{1,0:T(8,128)(2,1)}, f32[5,17,128]{2,1,0:T(8,128)}, f32[4,17,128]{2,1,0:T(8,128)}) custom-call(f32[3,4096]{1,0:T(4,128)} %refs_1_.1, f32[3,4096]{1,0:T(4,128)} %refs_2_.1, s32[8,4096]{1,0:T(8,128)} %far_edges.1, s32[1]{0:T(128)S(6)} %copy.12.far_counts, f32[1]{0:T(128)S(6)} %copy.11.far_sigma.refs_0_), custom_call_target="tpu_custom_call" | custom-call | flops 2300000000 | tf_op jit(solution)/shard_map/geometry/pallas_call | solution.py:505
  4.3 0.0 collective-permute-done.1.refs_8_
  4.4 0.0 collective-permute-done.refs_6_
  4.4 0.0 copy-start.1
  4.4 9.1 %score.1.state = f32[88,128]{1,0:T(8,128)} custom-call(f32[1]{0:T(128)S(6)} %copy.11.far_sigma.refs_0_, f32[3,4096]{1,0:T(4,128)} %refs_1_.1, f32[3,4096]{1,0:T(4,128)} %refs_2_.1, f32[3,2048]{1,0:T(4,128)} %refs_3_.1, s32[1,4096]{1,0:T(1,128)} %bitcast.2, bf16[64,4096]{1,0:T(8,128)(2,1)} %refs_5_.1, bf16[64,4096]{1,0:T(8,128)(2,1)} %collective-permute-done.refs_6_, ...), custom_call_target="tpu_custom_call" | custom-call | flops 11500000256 | tf_op jit(solution)/shard_map/score/pallas_call | solution.py:527
  13.5 3.0 %collective-permute-start.2 = (f32[88,128]{1,0:T(8,128)}, f32[88,128]{1,0:T(8,128)S(1)}, u32[]{:S(2)}, u32[]{:S(2)}) collective-permute-start(f32[88,128]{1,0:T(8,128)} %score.1.state), channel_id=1, source_target_pairs={{0,2},{2,0},{1,3},{3,1},{4,6},{6,4},{5,7},{7,5},{8,10},{10,8},{9,1... | collective-permute-start | bytes 135176 | tf_op jit(solution)/shard_map/ppermute | solution.py:483
  16.5 0.8 %copy-done = f32[88,128]{1,0:T(8,128)S(1)} copy-done((f32[88,128]{1,0:T(8,128)S(1)}, f32[88,128]{1,0:T(8,128)}, u32[]{:S(2)}) %copy-start) | copy-done | bytes 45080
  17.3 1.6 %collective-permute-start.6 = (bf16[240,128]{1,0:T(8,128)(2,1)S(1)}, bf16[240,128]{1,0:T(8,128)(2,1)S(1)}, u32[]{:S(2)}, u32[]{:S(2)}) collective-permute-start(bf16[240,128]{1,0:T(8,128)(2,1)S(1)} %get-tuple-element.18.refs_0_), channel_id=1, source_target_pairs={{0,4},{4,8},{8,12},{12,0},{1,5},{5,9},{9,13},{13,1},{2,6},{6,10},{... | collective-permute-start | bytes 184328 | tf_op jit(solution)/shard_map/ppermute | solution.py:483
  18.9 2.6 %collective-permute-start.7 = (bf16[240,128]{1,0:T(8,128)(2,1)S(1)}, bf16[240,128]{1,0:T(8,128)(2,1)S(1)}, u32[]{:S(2)}, u32[]{:S(2)}) collective-permute-start(bf16[240,128]{1,0:T(8,128)(2,1)S(1)} %get-tuple-element.18.refs_0_), channel_id=1, source_target_pairs={{0,8},{4,12},{8,0},{12,4},{1,9},{5,13},{9,1},{13,5},{2,10},{6,14},... | collective-permute-start | bytes 184328 | tf_op jit(solution)/shard_map/ppermute | solution.py:483
  21.5 1.4 %collective-permute-start.8 = (bf16[240,128]{1,0:T(8,128)(2,1)S(1)}, bf16[240,128]{1,0:T(8,128)(2,1)S(1)}, u32[]{:S(2)}, u32[]{:S(2)}) collective-permute-start(bf16[240,128]{1,0:T(8,128)(2,1)S(1)} %get-tuple-element.18.refs_0_), channel_id=1, source_target_pairs={{0,12},{4,0},{8,4},{12,8},{1,13},{5,1},{9,5},{13,9},{2,14},{6,2},{... | collective-permute-start | bytes 184328 | tf_op jit(solution)/shard_map/ppermute | solution.py:483
  22.9 0.0 collective-permute-done.2.refs_0_
  22.9 0.7 %collective-permute-start.3 = (f32[72,128]{1,0:T(8,128)S(1)}, f32[72,128]{1,0:T(8,128)S(1)}, u32[]{:S(2)}, u32[]{:S(2)}) collective-permute-start(f32[72,128]{1,0:T(8,128)S(1)} %get-tuple-element.17.refs_0_), channel_id=1, source_target_pairs={{0,4},{4,8},{8,12},{12,0},{1,5},{5,9},{9,13},{13,1},{2,6},{6,10},{... | collective-permute-start | bytes 110600 | tf_op jit(solution)/shard_map/ppermute | solution.py:483
  23.6 0.3 collective-permute-start.4
  24.0 2.8 %collective-permute-start.5 = (f32[72,128]{1,0:T(8,128)S(1)}, f32[72,128]{1,0:T(8,128)S(1)}, u32[]{:S(2)}, u32[]{:S(2)}) collective-permute-start(f32[72,128]{1,0:T(8,128)S(1)} %get-tuple-element.17.refs_0_), channel_id=1, source_target_pairs={{0,12},{4,0},{8,4},{12,8},{1,13},{5,1},{9,5},{13,9},{2,14},{6,2},{... | collective-permute-start | bytes 110600 | tf_op jit(solution)/shard_map/ppermute | solution.py:483
  26.8 1.3 %neighbours.1 = (s32[4,8,24,128]{3,2,1,0:T(8,128)S(1)}, s32[4,8,24,128]{3,2,1,0:T(8,128)S(1)}, f32[4,8,24,128]{3,2,1,0:T(8,128)S(1)}) custom-call(bf16[240,128]{1,0:T(8,128)(2,1)S(1)} %get-tuple-element.18.refs_0_, bf16[240,128]{1,0:T(8,128)(2,1)S(1)} %collective-permute-done.6.refs_1_, bf16[240,128]{1,0:T(8,128)(2,1)S(1)} %collective-permute-done.7.refs_2_, ...), custom_call_target="tpu_custom_call" | custom-call | flops 2300000000 | tf_op jit(solution)/shard_map/neighbours/pallas_call | solution.py:563
  28.1 0.7 %collective-permute-done.3.refs_1_ = f32[72,128]{1,0:T(8,128)S(1)} collective-permute-done((f32[72,128]{1,0:T(8,128)S(1)}, f32[72,128]{1,0:T(8,128)S(1)}, u32[]{:S(2)}, u32[]{:S(2)}) %collective-permute-start.3) | collective-permute-done | bytes 36896 | tf_op jit(solution)/shard_map/ppermute | solution.py:483
  28.8 0.8 %collective-permute-done.4.refs_2_ = f32[72,128]{1,0:T(8,128)S(1)} collective-permute-done((f32[72,128]{1,0:T(8,128)S(1)}, f32[72,128]{1,0:T(8,128)S(1)}, u32[]{:S(2)}, u32[]{:S(2)}) %collective-permute-start.4) | collective-permute-done | bytes 36896 | tf_op jit(solution)/shard_map/ppermute | solution.py:483
  29.6 4.6 %sweeps.1.part = f32[3,2048]{1,0:T(4,128)S(1)} custom-call(f32[72,128]{1,0:T(8,128)S(1)} %get-tuple-element.17.refs_0_, f32[72,128]{1,0:T(8,128)S(1)} %collective-permute-done.3.refs_1_, f32[72,128]{1,0:T(8,128)S(1)} %collective-permute-done.4.refs_2_, f32[72,128]{1,0:T(8,128)S(1)} %collective-permute-done.5.refs_3_, ...), custom_call_target="tpu_custom_call" | custom-call | flops 8049999872 | tf_op jit(solution)/shard_map/sweeps/pallas_call | solution.py:602
  34.2 0.1 collective-permute-start.9
  34.3 0.5 %collective-permute-start.10 = (f32[17,128]{1,0:T(8,128)S(1)}, f32[17,128]{1,0:T(8,128)S(1)}, u32[]{:S(2)}, u32[]{:S(2)}) collective-permute-start(f32[17,128]{1,0:T(8,128)S(1)} %get-tuple-element.23.mass), channel_id=1, source_target_pairs={{0,1},{1,0},{2,3},{3,2},{4,5},{5,4},{6,7},{7,6},{8,9},{9,8},{10,11... | collective-permute-start | bytes 26120 | tf_op jit(solution)/shard_map/ppermute | solution.py:483
  34.8 0.8 %collective-permute-done.10.mass_far = f32[17,128]{1,0:T(8,128)S(1)} collective-permute-done((f32[17,128]{1,0:T(8,128)S(1)}, f32[17,128]{1,0:T(8,128)S(1)}, u32[]{:S(2)}, u32[]{:S(2)}) %collective-permute-start.10) | collective-permute-done | bytes 8736 | tf_op jit(solution)/shard_map/ppermute | solution.py:483
  35.6 0.6 %whole.1 = (f32[3,4096]{1,0:T(4,128)}, f32[32,128]{1,0:T(8,128)}) custom-call(f32[3,2048]{1,0:T(4,128)S(1)} %sweeps.1.part, f32[3,2048]{1,0:T(4,128)S(1)} %collective-permute-done.9.part_far, f32[17,128]{1,0:T(8,128)S(1)} %get-tuple-element.23.mass, f32[17,128]{1,0:T(8,128)S(1)} %collective-permute-done.10.mass_far), custom_call_target="tpu_custom_call" | custom-call | flops 575000000 | tf_op jit(solution)/shard_map/whole/pallas_call | solution.py:619
  (13 shorter events, 0.1 us)
Async XLA Ops:
  0.6 3.7 %collective-permute-start = (bf16[64,4096]{1,0:T(8,128)(2,1)}, bf16[64,4096]{1,0:T(8,128)(2,1)}, u32[]{:S(2)}, u32[]{:S(2)}) collective-permute-start(bf16[64,4096]{1,0:T(8,128)(2,1)} %refs_5_.1), channel_id=1, source_target_pairs={{0,1},{1,0},{2,3},{3,2},{4,5},{5,4},{6,7},{7,6},{8,9},{9,8},{10,11... | collective-permute-start | bytes 1572872 | tf_op jit(solution)/shard_map/ppermute | solution.py:483
  1.1 3.2 %collective-permute-start.1 = (bf16[64,2048]{1,0:T(8,128)(2,1)}, bf16[64,2048]{1,0:T(8,128)(2,1)}, u32[]{:S(2)}, u32[]{:S(2)}) collective-permute-start(bf16[64,2048]{1,0:T(8,128)(2,1)} %refs_7_.1), channel_id=1, source_target_pairs={{0,1},{1,0},{2,3},{3,2},{4,5},{5,4},{6,7},{7,6},{8,9},{9,8},{10,11... | collective-permute-start | bytes 786440 | tf_op jit(solution)/shard_map/ppermute | solution.py:483
  4.4 12.1 %copy-start.1 = (bf16[240,128]{1,0:T(8,128)(2,1)S(1)}, bf16[240,128]{1,0:T(8,128)(2,1)}, u32[]{:S(2)}) copy-start(bf16[240,128]{1,0:T(8,128)(2,1)} %get-tuple-element.15.geo) | copy-start | bytes 184324
  4.4 12.1 %copy-start.2 = (f32[5,17,128]{2,1,0:T(8,128)S(1)}, f32[5,17,128]{2,1,0:T(8,128)}, u32[]{:S(2)}) copy-start(f32[5,17,128]{2,1,0:T(8,128)} %get-tuple-element.14.refs_9_.z_ref) | copy-start | bytes 130564
  13.5 9.4 %collective-permute-start.2 = (f32[88,128]{1,0:T(8,128)}, f32[88,128]{1,0:T(8,128)S(1)}, u32[]{:S(2)}, u32[]{:S(2)}) collective-permute-start(f32[88,128]{1,0:T(8,128)} %score.1.state), channel_id=1, source_target_pairs={{0,2},{2,0},{1,3},{3,1},{4,6},{6,4},{5,7},{7,5},{8,10},{10,8},{9,1... | collective-permute-start | bytes 135176 | tf_op jit(solution)/shard_map/ppermute | solution.py:483
  16.4 0.8 %copy-start = (f32[88,128]{1,0:T(8,128)S(1)}, f32[88,128]{1,0:T(8,128)}, u32[]{:S(2)}) copy-start(f32[88,128]{1,0:T(8,128)} %score.1.state) | copy-start | bytes 135172
  17.3 6.7 %collective-permute-start.6 = (bf16[240,128]{1,0:T(8,128)(2,1)S(1)}, bf16[240,128]{1,0:T(8,128)(2,1)S(1)}, u32[]{:S(2)}, u32[]{:S(2)}) collective-permute-start(bf16[240,128]{1,0:T(8,128)(2,1)S(1)} %get-tuple-element.18.refs_0_), channel_id=1, source_target_pairs={{0,4},{4,8},{8,12},{12,0},{1,5},{5,9},{9,13},{13,1},{2,6},{6,10},{... | collective-permute-start | bytes 184328 | tf_op jit(solution)/shard_map/ppermute | solution.py:483
  18.9 7.9 %collective-permute-start.7 = (bf16[240,128]{1,0:T(8,128)(2,1)S(1)}, bf16[240,128]{1,0:T(8,128)(2,1)S(1)}, u32[]{:S(2)}, u32[]{:S(2)}) collective-permute-start(bf16[240,128]{1,0:T(8,128)(2,1)S(1)} %get-tuple-element.18.refs_0_), channel_id=1, source_target_pairs={{0,8},{4,12},{8,0},{12,4},{1,9},{5,13},{9,1},{13,5},{2,10},{6,14},... | collective-permute-start | bytes 184328 | tf_op jit(solution)/shard_map/ppermute | solution.py:483
  21.5 5.3 %collective-permute-start.8 = (bf16[240,128]{1,0:T(8,128)(2,1)S(1)}, bf16[240,128]{1,0:T(8,128)(2,1)S(1)}, u32[]{:S(2)}, u32[]{:S(2)}) collective-permute-start(bf16[240,128]{1,0:T(8,128)(2,1)S(1)} %get-tuple-element.18.refs_0_), channel_id=1, source_target_pairs={{0,12},{4,0},{8,4},{12,8},{1,13},{5,1},{9,5},{13,9},{2,14},{6,2},{... | collective-permute-start | bytes 184328 | tf_op jit(solution)/shard_map/ppermute | solution.py:483
  22.9 6.7 %copy-start.3 = (f32[4,17,128]{2,1,0:T(8,128)S(1)}, f32[4,17,128]{2,1,0:T(8,128)}, u32[]{:S(2)}) copy-start(f32[4,17,128]{2,1,0:T(8,128)} %get-tuple-element.22.refs_7_) | copy-start | bytes 104452
  22.9 5.9 %collective-permute-start.3 = (f32[72,128]{1,0:T(8,128)S(1)}, f32[72,128]{1,0:T(8,128)S(1)}, u32[]{:S(2)}, u32[]{:S(2)}) collective-permute-start(f32[72,128]{1,0:T(8,128)S(1)} %get-tuple-element.17.refs_0_), channel_id=1, source_target_pairs={{0,4},{4,8},{8,12},{12,0},{1,5},{5,9},{9,13},{13,1},{2,6},{6,10},{... | collective-permute-start | bytes 110600 | tf_op jit(solution)/shard_map/ppermute | solution.py:483
  23.6 6.0 %collective-permute-start.4 = (f32[72,128]{1,0:T(8,128)S(1)}, f32[72,128]{1,0:T(8,128)S(1)}, u32[]{:S(2)}, u32[]{:S(2)}) collective-permute-start(f32[72,128]{1,0:T(8,128)S(1)} %get-tuple-element.17.refs_0_), channel_id=1, source_target_pairs={{0,8},{4,12},{8,0},{12,4},{1,9},{5,13},{9,1},{13,5},{2,10},{6,14},... | collective-permute-start | bytes 110600 | tf_op jit(solution)/shard_map/ppermute | solution.py:483
  24.0 5.7 %collective-permute-start.5 = (f32[72,128]{1,0:T(8,128)S(1)}, f32[72,128]{1,0:T(8,128)S(1)}, u32[]{:S(2)}, u32[]{:S(2)}) collective-permute-start(f32[72,128]{1,0:T(8,128)S(1)} %get-tuple-element.17.refs_0_), channel_id=1, source_target_pairs={{0,12},{4,0},{8,4},{12,8},{1,13},{5,1},{9,5},{13,9},{2,14},{6,2},{... | collective-permute-start | bytes 110600 | tf_op jit(solution)/shard_map/ppermute | solution.py:483
  34.2 1.4 %collective-permute-start.9 = (f32[3,2048]{1,0:T(4,128)S(1)}, f32[3,2048]{1,0:T(4,128)S(1)}, u32[]{:S(2)}, u32[]{:S(2)}) collective-permute-start(f32[3,2048]{1,0:T(4,128)S(1)} %sweeps.1.part), channel_id=1, source_target_pairs={{0,1},{1,0},{2,3},{3,2},{4,5},{5,4},{6,7},{7,6},{8,9},{9,8},{10,11... | collective-permute-start | bytes 73736 | tf_op jit(solution)/shard_map/ppermute | solution.py:483
  34.3 1.3 %collective-permute-start.10 = (f32[17,128]{1,0:T(8,128)S(1)}, f32[17,128]{1,0:T(8,128)S(1)}, u32[]{:S(2)}, u32[]{:S(2)}) collective-permute-start(f32[17,128]{1,0:T(8,128)S(1)} %get-tuple-element.23.mass), channel_id=1, source_target_pairs={{0,1},{1,0},{2,3},{3,2},{4,5},{5,4},{6,7},{7,6},{8,9},{9,8},{10,11... | collective-permute-start | bytes 26120 | tf_op jit(solution)/shard_map/ppermute | solution.py:483

commit v4 on v3

--- a/solution.py
+++ b/solution.py
@@ -54,18 +54,22 @@
     return copies
 
 
-def geometry_kernel(
-    far_pos, far_disp, far_edges, far_counts, far_sigma, geo, z_out, disp_out, src_pos, disp, edges, counts, sigma, rows, done
-):
+def hold_kernel(out):
+    out[...] = jnp.zeros_like(out)
+
+
+def bundle_places(blocks):
+    at_z = 8 * ((5 * blocks + 7) // 8)
+    at_geo = 2 * at_z
+    return at_z, at_geo, at_geo + 16 * ((14 * blocks + 15) // 16)
+
+
+def geometry(src_pos, disp, edges, counts, sigma, bundle, disp_out):
     slots = src_pos.shape[1]
     base = first_slot(slots)
-    blocks = z_out.shape[1]
-    copies = copies_in(
-        [far_pos, far_disp, far_edges, far_counts, far_sigma], [src_pos, disp, edges, counts, sigma], done
-    )
-    rows[...] = jnp.zeros_like(rows)
-    for copy in copies:
-        copy.wait()
+    blocks = disp_out.shape[1]
+    at_z, at_geo, _ = bundle_places(blocks)
+    bundle[...] = jnp.zeros_like(bundle)
     for at in range(blocks):
         here = pl.ds(pl.multiple_of(base + at * LANES, LANES), LANES)
         pos = src_pos[:, here]
@@ -80,35 +84,40 @@
         high = pos.astype(BF16).astype(F32)
         low = pos - high
         for k in range(EDGES):
-            rows[k * blocks + at : k * blocks + at + 1, :] = code[k : k + 1, :]
+            put = at_geo + k * blocks + at
+            bundle[put : put + 1, :] = code[k : k + 1, :]
         for c in range(3):
-            put = (EDGES + c) * blocks + at
-            rows[put : put + 1, :] = high[c : c + 1, :]
-            put = (EDGES + 3 + c) * blocks + at
-            rows[put : put + 1, :] = low[c : c + 1, :]
-            z_out[c, at : at + 1, :] = z[c : c + 1, :]
+            put = at_geo + (EDGES + c) * blocks + at
+            bundle[put : put + 1, :] = high[c : c + 1, :]
+            put = at_geo + (EDGES + 3 + c) * blocks + at
+            bundle[put : put + 1, :] = low[c : c + 1, :]
+            put = at_z + c * blocks + at
+            bundle[put : put + 1, :] = z[c : c + 1, :]
             disp_out[c, at : at + 1, :] = move[c : c + 1, :]
     live = (slot_ids(slots, blocks) < counts[0]).astype(F32)
-    z_out[3] = live
-    z_out[4] = jnp.full((blocks, LANES), sigma[0], F32)
+    bundle[at_z + 3 * blocks : at_z + 4 * blocks, :] = live
+    bundle[at_z + 4 * blocks : at_z + 5 * blocks, :] = jnp.full((blocks, LANES), sigma[0], F32)
     disp_out[3] = live
-    geo[...] = rows[...].astype(BF16)
 
 
 def score_kernel(*refs, chunk, tile):
-    far, state, near = refs[:9], refs[10], refs[11:20]
-    cols, aug, x_cols, left, score, highest, done = refs[20:]
+    far, near = refs[:11], refs[15:26]
+    state, bundle, disp_out = refs[12:15]
+    cols, aug, x_cols, left, score, highest, done = refs[26:]
     slots = far[1].shape[1]
     points = cols.shape[0]
     mine = pl.ds(pl.multiple_of(first_slot(slots), LANES), points)
-    sources = [*far[:5], far[5].at[:, mine], far[6].at[:, mine], far[7], far[8]]
+    sources = [*far[:7], far[7].at[:, mine], far[8].at[:, mine], far[9], far[10]]
     copies = copies_in(sources, near, done)
-    for copy in copies[:5]:
+    for copy in copies[:7]:
         copy.wait()
-    prepare(*near[:5], cols, aug, x_cols)
-    for copy in copies[5:]:
+    sigma, src_pos, disp, tgt_pos, seeds, edges, counts = near[:7]
+    prepare(sigma, src_pos, disp, tgt_pos, seeds, cols, aug, x_cols)
+    geometry(src_pos, disp, edges, counts, sigma, bundle, disp_out)
+    for copy in copies[7:]:
         copy.wait()
-    score_all(*near[5:], cols, aug, x_cols, state, left, score, highest, chunk=chunk, tile=tile)
+    score_all(*near[7:], cols, aug, x_cols, state, left, score, highest, chunk=chunk, tile=tile)
+    bundle[0 : state.shape[0], :] = state[...]
 
 
 def prepare(sigmas, src_pos, disp, tgt_pos, seeds, cols, aug, x_cols):
@@ -205,18 +214,19 @@
     return first_slot(slots) + LANES * rows + lane_ids(blocks)
 
 
-def own_kernel(state, z_ref, geo, out, geo_out):
-    geo_out[...] = geo[...]
-    blocks = z_ref.shape[1]
+def own_kernel(bundle, out, geo_out):
+    blocks = out.shape[1]
+    at_z, at_geo, end = bundle_places(blocks)
+    geo_out[...] = bundle[at_geo:end, :].astype(BF16)
     for q in range(5):
-        out[q] = state[q * blocks : (q + 1) * blocks, :]
-    z = [z_ref[c] for c in range(3)]
-    sigma = z_ref[4]
+        out[q] = bundle[q * blocks : (q + 1) * blocks, :]
+    z = [bundle[at_z + c * blocks : at_z + (c + 1) * blocks, :] for c in range(3)]
+    sigma = bundle[at_z + 4 * blocks : at_z + 5 * blocks, :]
     for c in range(3):
         out[5 + c] = z[c]
     norm = (z[0] * z[0] + z[1] * z[1] + z[2] * z[2]) * (0.5 / sigma)
     out[8] = (norm + outlier_level) * LOG2E
-    out[9] = z_ref[3]
+    out[9] = bundle[at_z + 3 * blocks : at_z + 4 * blocks, :]
     out[10] = sigma
 
 
@@ -500,38 +510,33 @@
 
     geo_rows = 16 * ((14 * blocks + 15) // 16)
     hbm = pl.BlockSpec(memory_space=pltpu.HBM)
-    own = (src_pos, displacement, edges)
-    scalars = [pltpu.SMEM((1,), jnp.int32), pltpu.SMEM((1,), F32)]
-    geo, z, disp = pl.pallas_call(
-        geometry_kernel,
-        name="geometry",
-        out_shape=(
-            jax.ShapeDtypeStruct((geo_rows, LANES), BF16),
-            jax.ShapeDtypeStruct((5, blocks, LANES), F32),
-            jax.ShapeDtypeStruct((4, blocks, LANES), F32),
-        ),
-        in_specs=[hbm] * 5,
-        out_specs=(VMEM,) * 3,
-        scratch_shapes=[pltpu.VMEM(array.shape, array.dtype) for array in own]
-        + scalars
-        + [pltpu.VMEM((geo_rows, LANES), F32), pltpu.SemaphoreType.DMA((5,))],
+    held = pl.pallas_call(
+        hold_kernel,
+        name="hold",
+        out_shape=jax.ShapeDtypeStruct((8, LANES), F32),
+        out_specs=VMEM,
         compiler_params=pltpu.CompilerParams(vmem_limit_bytes=(64 << 20) - (64 << 10)),
         cost_estimate=takes(2),
-    )(*own, counts, sigma_sq)
-    arrays = (src_pos, displacement, tgt_pos, seed_target.reshape(1, slots))
+    )()
+    arrays = (src_pos, displacement, tgt_pos, seed_target.reshape(1, slots), edges)
     features = (src_feat, src_other, tgt_feat, tgt_other)
     tile = 256
     state_rows = 8 * ((5 * blocks + 7) // 8)
     mine = pltpu.VMEM((src_feat.shape[0], points), BF16)
     theirs = pltpu.VMEM(tgt_feat.shape, BF16)
-    state = pl.pallas_call(
+    state, bundle, disp = pl.pallas_call(
         functools.partial(score_kernel, chunk=points // 8, tile=tile),
         name="score",
-        out_shape=jax.ShapeDtypeStruct((state_rows, LANES), F32),
-        in_specs=[hbm] * 9 + [pl.BlockSpec(memory_space=pl.ANY)],
-        out_specs=VMEM,
-        scratch_shapes=scalars[1:]
+        out_shape=(
+            jax.ShapeDtypeStruct((state_rows, LANES), F32),
+            jax.ShapeDtypeStruct((bundle_places(blocks)[2], LANES), F32),
+            jax.ShapeDtypeStruct((4, blocks, LANES), F32),
+        ),
+        in_specs=[hbm] * 11 + [pl.BlockSpec(memory_space=pl.ANY)],
+        out_specs=(VMEM,) * 3,
+        scratch_shapes=[pltpu.SMEM((1,), F32)]
         + [pltpu.VMEM(array.shape, array.dtype) for array in arrays]
+        + [pltpu.SMEM((1,), jnp.int32)]
         + [mine, mine, theirs, theirs]
         + [
             pltpu.VMEM((points, LANES), F32),
@@ -540,11 +545,11 @@
             pltpu.VMEM((points, 2 * LANES), BF16),
             pltpu.VMEM((cands // tile, points, tile), F32),
             pltpu.VMEM((points, LANES), F32),
-            pltpu.SemaphoreType.DMA((9,)),
+            pltpu.SemaphoreType.DMA((11,)),
         ],
         compiler_params=pltpu.CompilerParams(vmem_limit_bytes=60 << 20),
         cost_estimate=takes(10),
-    )(sigma_sq, *arrays, *features, z)
+    )(sigma_sq, *arrays, counts, *features, held)
 
     own, geo = pl.pallas_call(
         own_kernel,
@@ -553,11 +558,11 @@
             jax.ShapeDtypeStruct((11, blocks, LANES), F32),
             jax.ShapeDtypeStruct((geo_rows, LANES), BF16),
         ),
-        in_specs=[VMEM] * 3,
+        in_specs=[VMEM],
         out_specs=(VMEM, VMEM),
         compiler_params=small,
         cost_estimate=takes(0.5),
-    )(state, z, geo)
+    )(bundle)
     geos = around(geo, "strip")
     shape = (strips, EDGES, ROWS_WIN, LANES)
     index, segment, weight = pl.pallas_call(

time: 36.5 us -> 35.8 us (0.981)
  Pallas kernels: 17.4 us -> 16.5 us
    pallas_call x1, Pallas kernels: 1.81 us -> 0.6 us  [on_device(): pl.pallas_call(hold_kernel, name='hold', out_shape=jax.ShapeDtypeStruct((...]
    unnamed x8 -> x4, local copies, waits for them, and re-layouts: 0.83 us -> 0.94 us
  transfers between devices with their start and end apart: 11 -> 11, of which waited for: 3 -> 4; matrix products, arithmetic and copies ran while one was open for 0% -> 0% of each run, Pallas kernels for 9% -> 6%
where the time goes in v4:
time: 35.8 us; the launch traced here: 35.6 us
  Pallas kernels  16.5 us (46%)
  starting transfers between devices  13.5 us (38%)
  waiting for transfers between devices  2.72 us (8%)
  between operations  1.98 us (6%)
  local copies, waits for them, and re-layouts  0.94 us (3%)
    ppermute x11, starting transfers between devices, around(): lax.ppermute(array, axis, [(i, (i + d) % count) for i in range(count)])  13.5 us
    pallas_call x1, Pallas kernels, on_device(): pl.pallas_call(functools.partial(score_kernel, chunk=points // 8, tile=ti...  9.31 us
    pallas_call x1, Pallas kernels, on_device(): pl.pallas_call(functools.partial(sweep_kernel, strips=strips, blocks=bloc...  4.58 us
    ppermute x11, waiting for transfers between devices, around(): lax.ppermute(array, axis, [(i, (i + d) % count) for i in range(count)])  2.72 us
    pallas_call x1, Pallas kernels, on_device(): pl.pallas_call(functools.partial(kernels_kernel, strips=strips, blocks=bl...  1.31 us
    unnamed x4, local copies, waits for them, and re-layouts  0.94 us
  transfers between devices with their start and end apart: 11, of which 4 were waited for; matrix products, arithmetic and copies ran while one was open for 0% of the time, Pallas kernels for 6%

profile of v4, /device:TPU:0, one launch (start us, length us, event | category | flops | bytes accessed | tf_op | source)
XLA Modules:
  0.0 35.6 jit_solution(15999060567738197284)
XLA Ops:
  0.6 0.5 %collective-permute-start = (bf16[64,4096]{1,0:T(8,128)(2,1)}, bf16[64,4096]{1,0:T(8,128)(2,1)}, u32[]{:S(2)}, u32[]{:S(2)}) collective-permute-start(bf16[64,4096]{1,0:T(8,128)(2,1)} %refs_7_.1), channel_id=1, source_target_pairs={{0,1},{1,0},{2,3},{3,2},{4,5},{5,4},{6,7},{7,6},{8,9},{9,8},{10,11... | collective-permute-start | bytes 1572872 | tf_op jit(solution)/shard_map/ppermute | solution.py:493
  1.1 0.1 collective-permute-start.1
  2.5 0.6 %hold.1.refs_11_ = f32[8,128]{1,0:T(8,128)} custom-call(), custom_call_target="tpu_custom_call" | custom-call | flops 2300000000 | tf_op jit(solution)/shard_map/hold/pallas_call | solution.py:513
  3.1 0.3 collective-permute-done.1.refs_10_
  3.4 0.0 collective-permute-done.refs_8_
  3.4 9.3 %score.1 = (f32[88,128]{1,0:T(8,128)}, f32[416,128]{1,0:T(8,128)}, f32[4,17,128]{2,1,0:T(8,128)}) custom-call(f32[1]{0:T(128)S(6)} %copy.11.refs_0_, f32[3,4096]{1,0:T(4,128)} %refs_1_.1, f32[3,4096]{1,0:T(4,128)} %refs_2_.1, f32[3,2048]{1,0:T(4,128)} %refs_3_.1, s32[1,4096]{1,0:T(1,128)} %bitcast.2, s32[8,4096]{1,0:T(8,128)} %refs_5_.1, ...), custom_call_target="tpu_custom_call" | custom-call | flops 11500000256 | tf_op jit(solution)/shard_map/score/pallas_call | solution.py:527
  12.7 2.9 %collective-permute-start.2 = (f32[88,128]{1,0:T(8,128)}, f32[88,128]{1,0:T(8,128)S(1)}, u32[]{:S(2)}, u32[]{:S(2)}) collective-permute-start(f32[88,128]{1,0:T(8,128)} %get-tuple-element.16), channel_id=1, source_target_pairs={{0,2},{2,0},{1,3},{3,1},{4,6},{6,4},{5,7},{7,5},{8,10},{10,8},{9,1... | collective-permute-start | bytes 135176 | tf_op jit(solution)/shard_map/ppermute | solution.py:493
  15.6 0.9 %copy-done = f32[416,128]{1,0:T(8,128)S(1)} copy-done((f32[416,128]{1,0:T(8,128)S(1)}, f32[416,128]{1,0:T(8,128)}, u32[]{:S(2)}) %copy-start) | copy-done | bytes 213016
  16.6 1.6 %collective-permute-start.6 = (bf16[240,128]{1,0:T(8,128)(2,1)S(1)}, bf16[240,128]{1,0:T(8,128)(2,1)S(1)}, u32[]{:S(2)}, u32[]{:S(2)}) collective-permute-start(bf16[240,128]{1,0:T(8,128)(2,1)S(1)} %get-tuple-element.18.refs_0_), channel_id=1, source_target_pairs={{0,4},{4,8},{8,12},{12,0},{1,5},{5,9},{9,13},{13,1},{2,6},{6,10},{... | collective-permute-start | bytes 184328 | tf_op jit(solution)/shard_map/ppermute | solution.py:493
  18.2 2.6 %collective-permute-start.7 = (bf16[240,128]{1,0:T(8,128)(2,1)S(1)}, bf16[240,128]{1,0:T(8,128)(2,1)S(1)}, u32[]{:S(2)}, u32[]{:S(2)}) collective-permute-start(bf16[240,128]{1,0:T(8,128)(2,1)S(1)} %get-tuple-element.18.refs_0_), channel_id=1, source_target_pairs={{0,8},{4,12},{8,0},{12,4},{1,9},{5,13},{9,1},{13,5},{2,10},{6,14},... | collective-permute-start | bytes 184328 | tf_op jit(solution)/shard_map/ppermute | solution.py:493
  20.8 1.3 %collective-permute-start.8 = (bf16[240,128]{1,0:T(8,128)(2,1)S(1)}, bf16[240,128]{1,0:T(8,128)(2,1)S(1)}, u32[]{:S(2)}, u32[]{:S(2)}) collective-permute-start(bf16[240,128]{1,0:T(8,128)(2,1)S(1)} %get-tuple-element.18.refs_0_), channel_id=1, source_target_pairs={{0,12},{4,0},{8,4},{12,8},{1,13},{5,1},{9,5},{13,9},{2,14},{6,2},{... | collective-permute-start | bytes 184328 | tf_op jit(solution)/shard_map/ppermute | solution.py:493
  22.2 0.0 copy-start.1
  22.2 0.7 %collective-permute-start.3 = (f32[72,128]{1,0:T(8,128)S(1)}, f32[72,128]{1,0:T(8,128)S(1)}, u32[]{:S(2)}, u32[]{:S(2)}) collective-permute-start(f32[72,128]{1,0:T(8,128)S(1)} %get-tuple-element.17.refs_0_), channel_id=1, source_target_pairs={{0,4},{4,8},{8,12},{12,0},{1,5},{5,9},{9,13},{13,1},{2,6},{6,10},{... | collective-permute-start | bytes 110600 | tf_op jit(solution)/shard_map/ppermute | solution.py:493
  22.9 0.3 collective-permute-start.4
  23.3 0.0 collective-permute-done.6.refs_1_
  23.3 2.8 %collective-permute-start.5 = (f32[72,128]{1,0:T(8,128)S(1)}, f32[72,128]{1,0:T(8,128)S(1)}, u32[]{:S(2)}, u32[]{:S(2)}) collective-permute-start(f32[72,128]{1,0:T(8,128)S(1)} %get-tuple-element.17.refs_0_), channel_id=1, source_target_pairs={{0,12},{4,0},{8,4},{12,8},{1,13},{5,1},{9,5},{13,9},{2,14},{6,2},{... | collective-permute-start | bytes 110600 | tf_op jit(solution)/shard_map/ppermute | solution.py:493
  26.1 1.3 %neighbours.1 = (s32[4,8,24,128]{3,2,1,0:T(8,128)S(1)}, s32[4,8,24,128]{3,2,1,0:T(8,128)S(1)}, f32[4,8,24,128]{3,2,1,0:T(8,128)S(1)}) custom-call(bf16[240,128]{1,0:T(8,128)(2,1)S(1)} %get-tuple-element.18.refs_0_, bf16[240,128]{1,0:T(8,128)(2,1)S(1)} %collective-permute-done.6.refs_1_, bf16[240,128]{1,0:T(8,128)(2,1)S(1)} %collective-permute-done.7.refs_2_, ...), custom_call_target="tpu_custom_call" | custom-call | flops 2300000000 | tf_op jit(solution)/shard_map/neighbours/pallas_call | solution.py:568
  27.4 0.7 %collective-permute-done.3.refs_1_ = f32[72,128]{1,0:T(8,128)S(1)} collective-permute-done((f32[72,128]{1,0:T(8,128)S(1)}, f32[72,128]{1,0:T(8,128)S(1)}, u32[]{:S(2)}, u32[]{:S(2)}) %collective-permute-start.3) | collective-permute-done | bytes 36896 | tf_op jit(solution)/shard_map/ppermute | solution.py:493
  28.1 0.9 %collective-permute-done.4.refs_2_ = f32[72,128]{1,0:T(8,128)S(1)} collective-permute-done((f32[72,128]{1,0:T(8,128)S(1)}, f32[72,128]{1,0:T(8,128)S(1)}, u32[]{:S(2)}, u32[]{:S(2)}) %collective-permute-start.4) | collective-permute-done | bytes 36896 | tf_op jit(solution)/shard_map/ppermute | solution.py:493
  29.0 4.6 %sweeps.1.part = f32[3,2048]{1,0:T(4,128)S(1)} custom-call(f32[72,128]{1,0:T(8,128)S(1)} %get-tuple-element.17.refs_0_, f32[72,128]{1,0:T(8,128)S(1)} %collective-permute-done.3.refs_1_, f32[72,128]{1,0:T(8,128)S(1)} %collective-permute-done.4.refs_2_, f32[72,128]{1,0:T(8,128)S(1)} %collective-permute-done.5.refs_3_, ...), custom_call_target="tpu_custom_call" | custom-call | flops 8049999872 | tf_op jit(solution)/shard_map/sweeps/pallas_call | solution.py:607
  33.6 0.1 collective-permute-start.9
  33.7 0.5 %collective-permute-start.10 = (f32[17,128]{1,0:T(8,128)S(1)}, f32[17,128]{1,0:T(8,128)S(1)}, u32[]{:S(2)}, u32[]{:S(2)}) collective-permute-start(f32[17,128]{1,0:T(8,128)S(1)} %get-tuple-element.23.mass), channel_id=1, source_target_pairs={{0,1},{1,0},{2,3},{3,2},{4,5},{5,4},{6,7},{7,6},{8,9},{9,8},{10,11... | collective-permute-start | bytes 26120 | tf_op jit(solution)/shard_map/ppermute | solution.py:493
  34.2 0.8 %collective-permute-done.10.mass_far = f32[17,128]{1,0:T(8,128)S(1)} collective-permute-done((f32[17,128]{1,0:T(8,128)S(1)}, f32[17,128]{1,0:T(8,128)S(1)}, u32[]{:S(2)}, u32[]{:S(2)}) %collective-permute-start.10) | collective-permute-done | bytes 8736 | tf_op jit(solution)/shard_map/ppermute | solution.py:493
  35.0 0.6 %whole.1 = (f32[3,4096]{1,0:T(4,128)}, f32[32,128]{1,0:T(8,128)}) custom-call(f32[3,2048]{1,0:T(4,128)S(1)} %sweeps.1.part, f32[3,2048]{1,0:T(4,128)S(1)} %collective-permute-done.9.part_far, f32[17,128]{1,0:T(8,128)S(1)} %get-tuple-element.23.mass, f32[17,128]{1,0:T(8,128)S(1)} %collective-permute-done.10.mass_far), custom_call_target="tpu_custom_call" | custom-call | flops 575000000 | tf_op jit(solution)/shard_map/whole/pallas_call | solution.py:624
  (9 shorter events, 0.1 us)
Async XLA Ops:
  0.6 2.8 %collective-permute-start = (bf16[64,4096]{1,0:T(8,128)(2,1)}, bf16[64,4096]{1,0:T(8,128)(2,1)}, u32[]{:S(2)}, u32[]{:S(2)}) collective-permute-start(bf16[64,4096]{1,0:T(8,128)(2,1)} %refs_7_.1), channel_id=1, source_target_pairs={{0,1},{1,0},{2,3},{3,2},{4,5},{5,4},{6,7},{7,6},{8,9},{9,8},{10,11... | collective-permute-start | bytes 1572872 | tf_op jit(solution)/shard_map/ppermute | solution.py:493
  1.1 2.3 %collective-permute-start.1 = (bf16[64,2048]{1,0:T(8,128)(2,1)}, bf16[64,2048]{1,0:T(8,128)(2,1)}, u32[]{:S(2)}, u32[]{:S(2)}) collective-permute-start(bf16[64,2048]{1,0:T(8,128)(2,1)} %refs_9_.1), channel_id=1, source_target_pairs={{0,1},{1,0},{2,3},{3,2},{4,5},{5,4},{6,7},{7,6},{8,9},{9,8},{10,11... | collective-permute-start | bytes 786440 | tf_op jit(solution)/shard_map/ppermute | solution.py:493
  12.7 9.4 %collective-permute-start.2 = (f32[88,128]{1,0:T(8,128)}, f32[88,128]{1,0:T(8,128)S(1)}, u32[]{:S(2)}, u32[]{:S(2)}) collective-permute-start(f32[88,128]{1,0:T(8,128)} %get-tuple-element.16), channel_id=1, source_target_pairs={{0,2},{2,0},{1,3},{3,1},{4,6},{6,4},{5,7},{7,5},{8,10},{10,8},{9,1... | collective-permute-start | bytes 135176 | tf_op jit(solution)/shard_map/ppermute | solution.py:493
  15.6 0.9 %copy-start = (f32[416,128]{1,0:T(8,128)S(1)}, f32[416,128]{1,0:T(8,128)}, u32[]{:S(2)}) copy-start(f32[416,128]{1,0:T(8,128)} %get-tuple-element.14.bundle) | copy-start | bytes 638980
  16.6 6.7 %collective-permute-start.6 = (bf16[240,128]{1,0:T(8,128)(2,1)S(1)}, bf16[240,128]{1,0:T(8,128)(2,1)S(1)}, u32[]{:S(2)}, u32[]{:S(2)}) collective-permute-start(bf16[240,128]{1,0:T(8,128)(2,1)S(1)} %get-tuple-element.18.refs_0_), channel_id=1, source_target_pairs={{0,4},{4,8},{8,12},{12,0},{1,5},{5,9},{9,13},{13,1},{2,6},{6,10},{... | collective-permute-start | bytes 184328 | tf_op jit(solution)/shard_map/ppermute | solution.py:493
  18.2 7.9 %collective-permute-start.7 = (bf16[240,128]{1,0:T(8,128)(2,1)S(1)}, bf16[240,128]{1,0:T(8,128)(2,1)S(1)}, u32[]{:S(2)}, u32[]{:S(2)}) collective-permute-start(bf16[240,128]{1,0:T(8,128)(2,1)S(1)} %get-tuple-element.18.refs_0_), channel_id=1, source_target_pairs={{0,8},{4,12},{8,0},{12,4},{1,9},{5,13},{9,1},{13,5},{2,10},{6,14},... | collective-permute-start | bytes 184328 | tf_op jit(solution)/shard_map/ppermute | solution.py:493
  20.8 5.3 %collective-permute-start.8 = (bf16[240,128]{1,0:T(8,128)(2,1)S(1)}, bf16[240,128]{1,0:T(8,128)(2,1)S(1)}, u32[]{:S(2)}, u32[]{:S(2)}) collective-permute-start(bf16[240,128]{1,0:T(8,128)(2,1)S(1)} %get-tuple-element.18.refs_0_), channel_id=1, source_target_pairs={{0,12},{4,0},{8,4},{12,8},{1,13},{5,1},{9,5},{13,9},{2,14},{6,2},{... | collective-permute-start | bytes 184328 | tf_op jit(solution)/shard_map/ppermute | solution.py:493
  22.2 6.8 %copy-start.1 = (f32[4,17,128]{2,1,0:T(8,128)S(1)}, f32[4,17,128]{2,1,0:T(8,128)}, u32[]{:S(2)}) copy-start(f32[4,17,128]{2,1,0:T(8,128)} %get-tuple-element.22.refs_7_) | copy-start | bytes 104452
  22.2 5.9 %collective-permute-start.3 = (f32[72,128]{1,0:T(8,128)S(1)}, f32[72,128]{1,0:T(8,128)S(1)}, u32[]{:S(2)}, u32[]{:S(2)}) collective-permute-start(f32[72,128]{1,0:T(8,128)S(1)} %get-tuple-element.17.refs_0_), channel_id=1, source_target_pairs={{0,4},{4,8},{8,12},{12,0},{1,5},{5,9},{9,13},{13,1},{2,6},{6,10},{... | collective-permute-start | bytes 110600 | tf_op jit(solution)/shard_map/ppermute | solution.py:493
  22.9 6.1 %collective-permute-start.4 = (f32[72,128]{1,0:T(8,128)S(1)}, f32[72,128]{1,0:T(8,128)S(1)}, u32[]{:S(2)}, u32[]{:S(2)}) collective-permute-start(f32[72,128]{1,0:T(8,128)S(1)} %get-tuple-element.17.refs_0_), channel_id=1, source_target_pairs={{0,8},{4,12},{8,0},{12,4},{1,9},{5,13},{9,1},{13,5},{2,10},{6,14},... | collective-permute-start | bytes 110600 | tf_op jit(solution)/shard_map/ppermute | solution.py:493
  23.3 5.7 %collective-permute-start.5 = (f32[72,128]{1,0:T(8,128)S(1)}, f32[72,128]{1,0:T(8,128)S(1)}, u32[]{:S(2)}, u32[]{:S(2)}) collective-permute-start(f32[72,128]{1,0:T(8,128)S(1)} %get-tuple-element.17.refs_0_), channel_id=1, source_target_pairs={{0,12},{4,0},{8,4},{12,8},{1,13},{5,1},{9,5},{13,9},{2,14},{6,2},{... | collective-permute-start | bytes 110600 | tf_op jit(solution)/shard_map/ppermute | solution.py:493
  33.6 1.4 %collective-permute-start.9 = (f32[3,2048]{1,0:T(4,128)S(1)}, f32[3,2048]{1,0:T(4,128)S(1)}, u32[]{:S(2)}, u32[]{:S(2)}) collective-permute-start(f32[3,2048]{1,0:T(4,128)S(1)} %sweeps.1.part), channel_id=1, source_target_pairs={{0,1},{1,0},{2,3},{3,2},{4,5},{5,4},{6,7},{7,6},{8,9},{9,8},{10,11... | collective-permute-start | bytes 73736 | tf_op jit(solution)/shard_map/ppermute | solution.py:493
  33.7 1.3 %collective-permute-start.10 = (f32[17,128]{1,0:T(8,128)S(1)}, f32[17,128]{1,0:T(8,128)S(1)}, u32[]{:S(2)}, u32[]{:S(2)}) collective-permute-start(f32[17,128]{1,0:T(8,128)S(1)} %get-tuple-element.23.mass), channel_id=1, source_target_pairs={{0,1},{1,0},{2,3},{3,2},{4,5},{5,4},{6,7},{7,6},{8,9},{9,8},{10,11... | collective-permute-start | bytes 26120 | tf_op jit(solution)/shard_map/ppermute | solution.py:493

commit v5 on v4

--- a/solution.py
+++ b/solution.py
@@ -372,8 +372,8 @@
 
 def sweep_kernel(*refs, strips, blocks):
     terms = refs[:strips]
-    index, segment, weight, disp, out = refs[strips : strips + 5]
-    rows, base, raw, field, last_rows = refs[strips + 5 :]
+    index, segment, weight, disp, _, out = refs[strips : strips + 6]
+    rows, base, raw, field, last_rows = refs[strips + 6 :]
     me = lax.axis_index("strip")
     core = lax.axis_index("feat")
     groups = ROWS_WIN // 4
@@ -608,7 +608,7 @@
         functools.partial(sweep_kernel, strips=strips, blocks=blocks),
         name="sweeps",
         out_shape=jax.ShapeDtypeStruct((3, half), F32),
-        in_specs=[VMEM] * (strips + 4),
+        in_specs=[VMEM] * (strips + 4) + [pl.BlockSpec(memory_space=pl.ANY)],
         out_specs=VMEM,
         scratch_shapes=[
             pltpu.VMEM((ROWS_WIN + 16, LANES), F32),
@@ -619,7 +619,7 @@
         ],
         compiler_params=small,
         cost_estimate=takes(7),
-    )(*all_terms, index, segment, weight, disp)
+    )(*all_terms, index, segment, weight, disp, mass_far)
 
     new_disp, mass_whole = pl.pallas_call(
         whole_kernel,

time: 35.8 us -> 35.7 us (level)
  starting transfers between devices: 13.5 us -> 13 us
    ppermute x11, starting transfers between devices: 13.5 us -> 13 us  [around(): lax.ppermute(array, axis, [(i, (i + d) % count) for i in range(count)])]
where the time goes in v5:
time: 35.7 us; the launch traced here: 35.5 us
  Pallas kernels  16.5 us (46%)
  starting transfers between devices  13 us (36%)
  waiting for transfers between devices  3.06 us (9%)
  between operations  1.99 us (6%)
  local copies, waits for them, and re-layouts  0.94 us (3%)
    ppermute x11, starting transfers between devices, around(): lax.ppermute(array, axis, [(i, (i + d) % count) for i in range(count)])  13 us
    pallas_call x1, Pallas kernels, on_device(): pl.pallas_call(functools.partial(score_kernel, chunk=points // 8, tile=ti...  9.31 us
    pallas_call x1, Pallas kernels, on_device(): pl.pallas_call(functools.partial(sweep_kernel, strips=strips, blocks=bloc...  4.58 us
    ppermute x11, waiting for transfers between devices, around(): lax.ppermute(array, axis, [(i, (i + d) % count) for i in range(count)])  3.06 us
    pallas_call x1, Pallas kernels, on_device(): pl.pallas_call(functools.partial(kernels_kernel, strips=strips, blocks=bl...  1.32 us
    unnamed x4, local copies, waits for them, and re-layouts  0.94 us
  transfers between devices with their start and end apart: 11, of which 4 were waited for; matrix products, arithmetic and copies ran while one was open for 0% of the time, Pallas kernels for 6%

profile of v5, /device:TPU:0, one launch (start us, length us, event | category | flops | bytes accessed | tf_op | source)
XLA Modules:
  0.0 35.5 jit_solution(3049357356686337987)
XLA Ops:
  0.6 0.5 %collective-permute-start = (bf16[64,4096]{1,0:T(8,128)(2,1)}, bf16[64,4096]{1,0:T(8,128)(2,1)}, u32[]{:S(2)}, u32[]{:S(2)}) collective-permute-start(bf16[64,4096]{1,0:T(8,128)(2,1)} %refs_7_.1), channel_id=1, source_target_pairs={{0,1},{1,0},{2,3},{3,2},{4,5},{5,4},{6,7},{7,6},{8,9},{9,8},{10,11... | collective-permute-start | bytes 1572872 | tf_op jit(solution)/shard_map/ppermute | solution.py:493
  1.1 0.1 collective-permute-start.1
  2.5 0.6 %hold.1.refs_11_ = f32[8,128]{1,0:T(8,128)} custom-call(), custom_call_target="tpu_custom_call" | custom-call | flops 2300000000 | tf_op jit(solution)/shard_map/hold/pallas_call | solution.py:513
  3.1 0.3 collective-permute-done.1.refs_10_
  3.4 0.0 collective-permute-done.refs_8_
  3.4 9.3 %score.1 = (f32[88,128]{1,0:T(8,128)}, f32[416,128]{1,0:T(8,128)}, f32[4,17,128]{2,1,0:T(8,128)}) custom-call(f32[1]{0:T(128)S(6)} %copy.11.refs_0_, f32[3,4096]{1,0:T(4,128)} %refs_1_.1, f32[3,4096]{1,0:T(4,128)} %refs_2_.1, f32[3,2048]{1,0:T(4,128)} %refs_3_.1, s32[1,4096]{1,0:T(1,128)} %bitcast.2, s32[8,4096]{1,0:T(8,128)} %refs_5_.1, ...), custom_call_target="tpu_custom_call" | custom-call | flops 11500000256 | tf_op jit(solution)/shard_map/score/pallas_call | solution.py:527
  12.7 2.9 %collective-permute-start.2 = (f32[88,128]{1,0:T(8,128)}, f32[88,128]{1,0:T(8,128)S(1)}, u32[]{:S(2)}, u32[]{:S(2)}) collective-permute-start(f32[88,128]{1,0:T(8,128)} %get-tuple-element.16), channel_id=1, source_target_pairs={{0,2},{2,0},{1,3},{3,1},{4,6},{6,4},{5,7},{7,5},{8,10},{10,8},{9,1... | collective-permute-start | bytes 135176 | tf_op jit(solution)/shard_map/ppermute | solution.py:493
  15.6 0.9 %copy-done = f32[416,128]{1,0:T(8,128)S(1)} copy-done((f32[416,128]{1,0:T(8,128)S(1)}, f32[416,128]{1,0:T(8,128)}, u32[]{:S(2)}) %copy-start) | copy-done | bytes 213016
  16.6 1.6 %collective-permute-start.6 = (bf16[240,128]{1,0:T(8,128)(2,1)S(1)}, bf16[240,128]{1,0:T(8,128)(2,1)S(1)}, u32[]{:S(2)}, u32[]{:S(2)}) collective-permute-start(bf16[240,128]{1,0:T(8,128)(2,1)S(1)} %get-tuple-element.18.refs_0_), channel_id=1, source_target_pairs={{0,4},{4,8},{8,12},{12,0},{1,5},{5,9},{9,13},{13,1},{2,6},{6,10},{... | collective-permute-start | bytes 184328 | tf_op jit(solution)/shard_map/ppermute | solution.py:493
  18.2 2.6 %collective-permute-start.7 = (bf16[240,128]{1,0:T(8,128)(2,1)S(1)}, bf16[240,128]{1,0:T(8,128)(2,1)S(1)}, u32[]{:S(2)}, u32[]{:S(2)}) collective-permute-start(bf16[240,128]{1,0:T(8,128)(2,1)S(1)} %get-tuple-element.18.refs_0_), channel_id=1, source_target_pairs={{0,8},{4,12},{8,0},{12,4},{1,9},{5,13},{9,1},{13,5},{2,10},{6,14},... | collective-permute-start | bytes 184328 | tf_op jit(solution)/shard_map/ppermute | solution.py:493
  20.8 1.3 %collective-permute-start.8 = (bf16[240,128]{1,0:T(8,128)(2,1)S(1)}, bf16[240,128]{1,0:T(8,128)(2,1)S(1)}, u32[]{:S(2)}, u32[]{:S(2)}) collective-permute-start(bf16[240,128]{1,0:T(8,128)(2,1)S(1)} %get-tuple-element.18.refs_0_), channel_id=1, source_target_pairs={{0,12},{4,0},{8,4},{12,8},{1,13},{5,1},{9,5},{13,9},{2,14},{6,2},{... | collective-permute-start | bytes 184328 | tf_op jit(solution)/shard_map/ppermute | solution.py:493
  22.2 0.0 collective-permute-done.2.refs_0_
  22.2 0.7 %collective-permute-start.3 = (f32[72,128]{1,0:T(8,128)S(1)}, f32[72,128]{1,0:T(8,128)S(1)}, u32[]{:S(2)}, u32[]{:S(2)}) collective-permute-start(f32[72,128]{1,0:T(8,128)S(1)} %get-tuple-element.17.refs_0_), channel_id=1, source_target_pairs={{0,4},{4,8},{8,12},{12,0},{1,5},{5,9},{9,13},{13,1},{2,6},{6,10},{... | collective-permute-start | bytes 110600 | tf_op jit(solution)/shard_map/ppermute | solution.py:493
  22.9 0.3 collective-permute-start.4
  23.3 0.0 collective-permute-done.6.refs_1_
  23.3 2.8 %collective-permute-start.5 = (f32[72,128]{1,0:T(8,128)S(1)}, f32[72,128]{1,0:T(8,128)S(1)}, u32[]{:S(2)}, u32[]{:S(2)}) collective-permute-start(f32[72,128]{1,0:T(8,128)S(1)} %get-tuple-element.17.refs_0_), channel_id=1, source_target_pairs={{0,12},{4,0},{8,4},{12,8},{1,13},{5,1},{9,5},{13,9},{2,14},{6,2},{... | collective-permute-start | bytes 110600 | tf_op jit(solution)/shard_map/ppermute | solution.py:493
  26.1 0.0 collective-permute-done.8.refs_3_
  26.1 1.3 %neighbours.1 = (s32[4,8,24,128]{3,2,1,0:T(8,128)S(1)}, s32[4,8,24,128]{3,2,1,0:T(8,128)S(1)}, f32[4,8,24,128]{3,2,1,0:T(8,128)S(1)}) custom-call(bf16[240,128]{1,0:T(8,128)(2,1)S(1)} %get-tuple-element.18.refs_0_, bf16[240,128]{1,0:T(8,128)(2,1)S(1)} %collective-permute-done.6.refs_1_, bf16[240,128]{1,0:T(8,128)(2,1)S(1)} %collective-permute-done.7.refs_2_, ...), custom_call_target="tpu_custom_call" | custom-call | flops 2300000000 | tf_op jit(solution)/shard_map/neighbours/pallas_call | solution.py:568
  27.4 0.7 %collective-permute-done.3.refs_1_ = f32[72,128]{1,0:T(8,128)S(1)} collective-permute-done((f32[72,128]{1,0:T(8,128)S(1)}, f32[72,128]{1,0:T(8,128)S(1)}, u32[]{:S(2)}, u32[]{:S(2)}) %collective-permute-start.3) | collective-permute-done | bytes 36896 | tf_op jit(solution)/shard_map/ppermute | solution.py:493
  28.1 0.9 %collective-permute-done.4.refs_2_ = f32[72,128]{1,0:T(8,128)S(1)} collective-permute-done((f32[72,128]{1,0:T(8,128)S(1)}, f32[72,128]{1,0:T(8,128)S(1)}, u32[]{:S(2)}, u32[]{:S(2)}) %collective-permute-start.4) | collective-permute-done | bytes 36896 | tf_op jit(solution)/shard_map/ppermute | solution.py:493
  29.0 4.6 %sweeps.1.part = f32[3,2048]{1,0:T(4,128)S(1)} custom-call(f32[72,128]{1,0:T(8,128)S(1)} %get-tuple-element.17.refs_0_, f32[72,128]{1,0:T(8,128)S(1)} %collective-permute-done.3.refs_1_, f32[72,128]{1,0:T(8,128)S(1)} %collective-permute-done.4.refs_2_, f32[72,128]{1,0:T(8,128)S(1)} %collective-permute-done.5.refs_3_, ...), custom_call_target="tpu_custom_call" | custom-call | flops 8049999872 | tf_op jit(solution)/shard_map/sweeps/pallas_call | solution.py:607
  33.6 0.1 collective-permute-start.10
  33.7 1.2 %collective-permute-done.10.part_far = f32[3,2048]{1,0:T(4,128)S(1)} collective-permute-done((f32[3,2048]{1,0:T(4,128)S(1)}, f32[3,2048]{1,0:T(4,128)S(1)}, u32[]{:S(2)}, u32[]{:S(2)}) %collective-permute-start.10) | collective-permute-done | bytes 24608 | tf_op jit(solution)/shard_map/ppermute | solution.py:493
  34.9 0.6 %whole.1 = (f32[3,4096]{1,0:T(4,128)}, f32[32,128]{1,0:T(8,128)}) custom-call(f32[3,2048]{1,0:T(4,128)S(1)} %sweeps.1.part, f32[3,2048]{1,0:T(4,128)S(1)} %collective-permute-done.10.part_far, f32[17,128]{1,0:T(8,128)S(1)} %get-tuple-element.23.mass, f32[17,128]{1,0:T(8,128)S(1)} %collective-permute-done.9.refs_8_.mass_far), custom_call_target="tpu_custom_call" | custom-call | flops 575000000 | tf_op jit(solution)/shard_map/whole/pallas_call | solution.py:624
  (9 shorter events, 0.1 us)
Async XLA Ops:
  0.6 2.8 %collective-permute-start = (bf16[64,4096]{1,0:T(8,128)(2,1)}, bf16[64,4096]{1,0:T(8,128)(2,1)}, u32[]{:S(2)}, u32[]{:S(2)}) collective-permute-start(bf16[64,4096]{1,0:T(8,128)(2,1)} %refs_7_.1), channel_id=1, source_target_pairs={{0,1},{1,0},{2,3},{3,2},{4,5},{5,4},{6,7},{7,6},{8,9},{9,8},{10,11... | collective-permute-start | bytes 1572872 | tf_op jit(solution)/shard_map/ppermute | solution.py:493
  1.1 2.3 %collective-permute-start.1 = (bf16[64,2048]{1,0:T(8,128)(2,1)}, bf16[64,2048]{1,0:T(8,128)(2,1)}, u32[]{:S(2)}, u32[]{:S(2)}) collective-permute-start(bf16[64,2048]{1,0:T(8,128)(2,1)} %refs_9_.1), channel_id=1, source_target_pairs={{0,1},{1,0},{2,3},{3,2},{4,5},{5,4},{6,7},{7,6},{8,9},{9,8},{10,11... | collective-permute-start | bytes 786440 | tf_op jit(solution)/shard_map/ppermute | solution.py:493
  12.7 9.4 %collective-permute-start.2 = (f32[88,128]{1,0:T(8,128)}, f32[88,128]{1,0:T(8,128)S(1)}, u32[]{:S(2)}, u32[]{:S(2)}) collective-permute-start(f32[88,128]{1,0:T(8,128)} %get-tuple-element.16), channel_id=1, source_target_pairs={{0,2},{2,0},{1,3},{3,1},{4,6},{6,4},{5,7},{7,5},{8,10},{10,8},{9,1... | collective-permute-start | bytes 135176 | tf_op jit(solution)/shard_map/ppermute | solution.py:493
  15.6 0.9 %copy-start = (f32[416,128]{1,0:T(8,128)S(1)}, f32[416,128]{1,0:T(8,128)}, u32[]{:S(2)}) copy-start(f32[416,128]{1,0:T(8,128)} %get-tuple-element.14.bundle) | copy-start | bytes 638980
  16.6 6.7 %collective-permute-start.6 = (bf16[240,128]{1,0:T(8,128)(2,1)S(1)}, bf16[240,128]{1,0:T(8,128)(2,1)S(1)}, u32[]{:S(2)}, u32[]{:S(2)}) collective-permute-start(bf16[240,128]{1,0:T(8,128)(2,1)S(1)} %get-tuple-element.18.refs_0_), channel_id=1, source_target_pairs={{0,4},{4,8},{8,12},{12,0},{1,5},{5,9},{9,13},{13,1},{2,6},{6,10},{... | collective-permute-start | bytes 184328 | tf_op jit(solution)/shard_map/ppermute | solution.py:493
  18.2 7.9 %collective-permute-start.7 = (bf16[240,128]{1,0:T(8,128)(2,1)S(1)}, bf16[240,128]{1,0:T(8,128)(2,1)S(1)}, u32[]{:S(2)}, u32[]{:S(2)}) collective-permute-start(bf16[240,128]{1,0:T(8,128)(2,1)S(1)} %get-tuple-element.18.refs_0_), channel_id=1, source_target_pairs={{0,8},{4,12},{8,0},{12,4},{1,9},{5,13},{9,1},{13,5},{2,10},{6,14},... | collective-permute-start | bytes 184328 | tf_op jit(solution)/shard_map/ppermute | solution.py:493
  20.8 5.3 %collective-permute-start.8 = (bf16[240,128]{1,0:T(8,128)(2,1)S(1)}, bf16[240,128]{1,0:T(8,128)(2,1)S(1)}, u32[]{:S(2)}, u32[]{:S(2)}) collective-permute-start(bf16[240,128]{1,0:T(8,128)(2,1)S(1)} %get-tuple-element.18.refs_0_), channel_id=1, source_target_pairs={{0,12},{4,0},{8,4},{12,8},{1,13},{5,1},{9,5},{13,9},{2,14},{6,2},{... | collective-permute-start | bytes 184328 | tf_op jit(solution)/shard_map/ppermute | solution.py:493
  22.2 5.9 %collective-permute-start.3 = (f32[72,128]{1,0:T(8,128)S(1)}, f32[72,128]{1,0:T(8,128)S(1)}, u32[]{:S(2)}, u32[]{:S(2)}) collective-permute-start(f32[72,128]{1,0:T(8,128)S(1)} %get-tuple-element.17.refs_0_), channel_id=1, source_target_pairs={{0,4},{4,8},{8,12},{12,0},{1,5},{5,9},{9,13},{13,1},{2,6},{6,10},{... | collective-permute-start | bytes 110600 | tf_op jit(solution)/shard_map/ppermute | solution.py:493
  22.9 6.1 %collective-permute-start.4 = (f32[72,128]{1,0:T(8,128)S(1)}, f32[72,128]{1,0:T(8,128)S(1)}, u32[]{:S(2)}, u32[]{:S(2)}) collective-permute-start(f32[72,128]{1,0:T(8,128)S(1)} %get-tuple-element.17.refs_0_), channel_id=1, source_target_pairs={{0,8},{4,12},{8,0},{12,4},{1,9},{5,13},{9,1},{13,5},{2,10},{6,14},... | collective-permute-start | bytes 110600 | tf_op jit(solution)/shard_map/ppermute | solution.py:493
  23.3 5.7 %collective-permute-start.5 = (f32[72,128]{1,0:T(8,128)S(1)}, f32[72,128]{1,0:T(8,128)S(1)}, u32[]{:S(2)}, u32[]{:S(2)}) collective-permute-start(f32[72,128]{1,0:T(8,128)S(1)} %get-tuple-element.17.refs_0_), channel_id=1, source_target_pairs={{0,12},{4,0},{8,4},{12,8},{1,13},{5,1},{9,5},{13,9},{2,14},{6,2},{... | collective-permute-start | bytes 110600 | tf_op jit(solution)/shard_map/ppermute | solution.py:493
  26.1 2.9 %copy-start.1 = (f32[4,17,128]{2,1,0:T(8,128)S(1)}, f32[4,17,128]{2,1,0:T(8,128)}, u32[]{:S(2)}) copy-start(f32[4,17,128]{2,1,0:T(8,128)} %get-tuple-element.22.refs_7_) | copy-start | bytes 104452
  26.1 1.3 %collective-permute-start.9 = (f32[17,128]{1,0:T(8,128)S(1)}, f32[17,128]{1,0:T(8,128)S(1)}, u32[]{:S(2)}, u32[]{:S(2)}) collective-permute-start(f32[17,128]{1,0:T(8,128)S(1)} %get-tuple-element.23.mass), channel_id=1, source_target_pairs={{0,1},{1,0},{2,3},{3,2},{4,5},{5,4},{6,7},{7,6},{8,9},{9,8},{10,11... | collective-permute-start | bytes 26120 | tf_op jit(solution)/shard_map/ppermute | solution.py:493
  33.6 1.3 %collective-permute-start.10 = (f32[3,2048]{1,0:T(4,128)S(1)}, f32[3,2048]{1,0:T(4,128)S(1)}, u32[]{:S(2)}, u32[]{:S(2)}) collective-permute-start(f32[3,2048]{1,0:T(4,128)S(1)} %sweeps.1.part), channel_id=1, source_target_pairs={{0,1},{1,0},{2,3},{3,2},{4,5},{5,4},{6,7},{7,6},{8,9},{9,8},{10,11... | collective-permute-start | bytes 73736 | tf_op jit(solution)/shard_map/ppermute | solution.py:493
